TPU v7x, 32 devices: a whole 2x2x4 slice. The times are simulated.
32 devices in a mesh: lat: 4 (over y, x), lon: 8 (over z, core).
Axes of the slice: x: 2, y: 2, z: 4, core: 2. Of those that a mesh axis runs over, the one named last changes fastest.
Arguments:
- ensemble: float32 [16, 64, 1792], P('lat', 'lon'), may hold values from -6 to 6
- northward_wind: float32 [16, 64], P('lat', 'lon'), may hold values from -1 to 1
- eastward_wind: float32 [16, 64], P('lat', 'lon'), may hold values from -1 to 1
- spreading_strength: float32 [16, 64], P('lat', 'lon'), may hold values from 0.05 to 0.2
- measurement_home_subdomain: int32 [3, 128], replicated, may hold values from 0 to 31, as said below
- obs_site: int32 [3, 128], replicated, may hold values from 0 to 895
- obs_class: int32 [3, 128], replicated, may hold values from 0 to 7
- cutoff_table: int32 [8], replicated, may hold values from 6 to 23
- obs_value: float32 [3, 128], replicated, may hold values from -6 to 6
- obs_var: float32 [3, 128], replicated, may hold values from 0.5 to 2
- obs_noise: float32 [3, 128, 64], replicated, may hold values from -6 to 6
Outputs:
- analysis: float32 [16, 64, 1792], P('lat', 'lon')
Inputs may be any that keep to these rules, and one draw needn't show every extreme that they name: `measurement_home_subdomain`: tile index is lat index * 8 + lon index; in every batch no tile owns more than 4 observations and some tile owns exactly 4.
All inputs are finite; a program needn't handle non-finite values.
Results may differ from a plain program's by a relative error of at most 0.0003.
Values sent between devices are 32-bit elements; how exact they have to be, the bound alone decides.
A program may use at most 64 MiB of HBM per device.

v0:
```python
import jax
import jax.numpy as jnp
from jax import lax
from jax.sharding import PartitionSpec as P

LEV = 28
MEMBERS = 64
SECTIONS = 2
BATCH_GROUPS = 3
CAP = 4


advect_coef = 0.2


def with_halo(block, sides, width, periodic):
    for axis, dim in sides:
        count = lax.axis_size(axis)
        forward = [(i, i + 1) for i in range(count - 1)]
        if periodic:
            forward.append((count - 1, 0))
        backward = [(target, source) for source, target in forward]
        low = lax.ppermute(
            lax.slice_in_dim(block, block.shape[dim] - width, None, axis=dim), axis, forward
        )
        high = lax.ppermute(lax.slice_in_dim(block, 0, width, axis=dim), axis, backward)
        block = jnp.concatenate([low, block, high], axis=dim)
    return block


def taper(dist, radius):
    z = dist / radius
    inner = 1.0 - 5.0 / 3.0 * z**2 + 0.625 * z**3 + 0.5 * z**4 - 0.25 * z**5
    outside = jnp.maximum(z, 1.0)
    outer = (
        4.0
        - 5.0 * outside
        + 5.0 / 3.0 * outside**2
        + 0.625 * outside**3
        - 0.5 * outside**4
        + outside**5 / 12.0
        - 2.0 / (3.0 * outside)
    )
    return jnp.where(z <= 1.0, inner, jnp.where(z < 2.0, outer, jnp.float32(0.0)))


def advance_subdomains(prognostic_fields, northward_wind, eastward_wind, spreading_strength):
    padded_lat = with_halo(prognostic_fields, (("lat", 0),), 1, False)
    padded_lon = with_halo(prognostic_fields, (("lon", 1),), 1, True)
    north = padded_lat[2:]
    south = padded_lat[:-2]
    east = padded_lon[:, 2:]
    west = padded_lon[:, :-2]
    lap = north + south + east + west - 4.0 * prognostic_fields
    return (
        prognostic_fields
        + spreading_strength[:, :, None] * lap
        - advect_coef
        * (northward_wind[:, :, None] * (north - south) + eastward_wind[:, :, None] * (east - west))
    )


def whiten(prior, value, var, noise):
    mean = jnp.mean(prior, axis=1, keepdims=True)
    anom = prior - mean
    cov = jnp.dot(anom, anom.T, precision=lax.Precision.HIGHEST) / jnp.float32(
        MEMBERS - 1
    ) + jnp.diag(var)
    factor = jnp.linalg.cholesky(cov)
    rhs = value[:, None] + jnp.sqrt(var)[:, None] * noise - prior
    return (anom, jax.scipy.linalg.cho_solve((factor, True), rhs))


def body(
    ensemble,
    northward_wind,
    eastward_wind,
    spreading_strength,
    measurement_home_subdomain,
    obs_site,
    obs_class,
    cutoff_table,
    obs_value,
    obs_var,
    obs_noise,
):
    tile_lat = ensemble.shape[0]
    tile_lon = ensemble.shape[1]
    lon_tiles = lax.axis_size("lon")
    lon_cells = tile_lon * lon_tiles
    row_base = lax.axis_index("lat") * tile_lat
    leading_column_offset = lax.axis_index("lon") * tile_lon
    myself = lax.axis_index("lat") * lon_tiles + lax.axis_index("lon")
    count = measurement_home_subdomain.shape[1]
    block = min(count, 128)
    prognostic_fields = ensemble
    for section in range(SECTIONS):
        prognostic_fields = advance_subdomains(
            prognostic_fields, northward_wind, eastward_wind, spreading_strength
        )
    lat_cells = row_base + jnp.arange(tile_lat, dtype=jnp.int32)
    lon_local = leading_column_offset + jnp.arange(tile_lon, dtype=jnp.int32)
    classes = jnp.arange(cutoff_table.shape[0], dtype=jnp.int32)
    for k in range(BATCH_GROUPS):
        owner = measurement_home_subdomain[k]
        site = obs_site[k]
        cell = site // LEV
        glat = owner // lon_tiles * tile_lat + cell // tile_lon
        glon = owner % lon_tiles * tile_lon + cell % tile_lon
        flat = prognostic_fields.reshape(-1, MEMBERS)
        picked = jnp.take(flat, site, axis=0)
        mine = owner == myself
        order_ids = jnp.arange(count, dtype=jnp.int32)
        earlier = (owner[:, None] == owner[None, :]) & (order_ids[:, None] < order_ids[None, :])
        rank = jnp.sum(earlier.astype(jnp.int32), axis=0)
        slots = jnp.arange(CAP, dtype=jnp.int32)
        select_rows = (mine[None, :] & (rank[None, :] == slots[:, None])).astype(jnp.float32)
        packed = jnp.dot(select_rows, picked, precision=lax.Precision.HIGHEST)
        gathered = lax.all_gather(packed, ("lat", "lon"), axis=0, tiled=True)
        prior = jnp.take(gathered, owner * CAP + rank, axis=0)
        anom_obs, white = whiten(prior, obs_value[k], obs_var[k], obs_noise[k])
        match = (obs_class[k][:, None] == classes[None, :]).astype(jnp.int32)
        radius = jnp.sum(match * cutoff_table[None, :], axis=1).astype(jnp.float32)
        dlat = jnp.abs(lat_cells[:, None] - glat[None, :]).astype(jnp.float32)
        dlon = jnp.abs(lon_local[:, None] - glon[None, :])
        dlon = jnp.minimum(dlon, lon_cells - dlon).astype(jnp.float32)
        dist = jnp.sqrt(dlat[:, None, :] * dlat[:, None, :] + dlon[None, :, :] * dlon[None, :, :])
        rho = taper(dist, radius[None, None, :]).reshape(tile_lat * tile_lon, count)
        cube = prognostic_fields.reshape(tile_lat * tile_lon, LEV, MEMBERS)
        xp = cube - jnp.mean(cube, axis=2, keepdims=True)
        total = jnp.zeros_like(cube)
        for start in range(0, count, block):
            part_anom = anom_obs[start : start + block]
            part_white = white[start : start + block]
            cov = jnp.einsum(
                "clm,jm->clj", xp, part_anom, precision=lax.Precision.HIGHEST
            ) / jnp.float32(MEMBERS - 1)
            total = total + jnp.einsum(
                "clj,jm->clm",
                cov * rho[:, None, start : start + block],
                part_white,
                precision=lax.Precision.HIGHEST,
            )
        prognostic_fields = (cube + total).reshape(tile_lat, tile_lon, LEV * MEMBERS)
    return prognostic_fields


def solution(mesh):
    placed = (
        P("lat", "lon", None),
        P("lat", "lon"),
        P("lat", "lon"),
        P("lat", "lon"),
        P(),
        P(),
        P(),
        P(),
        P(),
        P(),
        P(),
    )
    return jax.shard_map(
        body, mesh=mesh, in_specs=placed, out_specs=P("lat", "lon", None), check_vma=False
    )
```

profile of v0, /device:TPU:0, one launch (start us, length us, event | category | flops | bytes accessed | tf_op | source)
XLA Modules:
  0.0 227.1 jit_solution(4815321617645588931)
XLA Ops:
  0.0 0.9 fusion.202
  0.9 1.3 collective-permute-start
  2.2 5.6 %collective-permute-start.1 = (f32[1,8,1792]{2,1,0:T(8,128)S(1)}, f32[1,8,1792]{2,1,0:T(8,128)S(1)}, u32[]{:S(2)}, u32[]{:S(2)}) collective-permute-start(f32[1,8,1792]{2,1,0:T(8,128)S(1)} %get-tuple-element.34), channel_id=1, source_target_pairs={{0,8},{8,16},{16,24},{1,9},{9,17},{17,25},{2,10},{10,18},{18,26},{... | collective-permute-start | bytes 172040 | tf_op jit(solution)/shard_map/ppermute | solution.py:23
  7.9 3.1 %collective-permute-start.2 = (f32[4,1,1792]{2,1,0:T(1,128)S(1)}, f32[4,1,1792]{2,1,0:T(1,128)S(1)}, u32[]{:S(2)}, u32[]{:S(2)}) collective-permute-start(f32[4,1,1792]{2,1,0:T(1,128)S(1)} %get-tuple-element.36), channel_id=1, source_target_pairs={{1,0},{2,1},{3,2},{4,3},{5,4},{6,5},{7,6},{0,7},{9,8},{10,9},{11,1... | collective-permute-start | bytes 86024 | tf_op jit(solution)/shard_map/ppermute | solution.py:26
  11.7 0.7 copy-done.2
  13.4 0.7 copy-done.9
  15.2 0.9 collective-permute-done.3
  16.3 1.3 collective-permute-start.4
  17.6 4.9 %collective-permute-start.5 = (f32[1,8,1792]{2,1,0:T(8,128)S(1)}, f32[1,8,1792]{2,1,0:T(8,128)S(1)}, u32[]{:S(2)}, u32[]{:S(2)}) collective-permute-start(f32[1,8,1792]{2,1,0:T(8,128)S(1)} %get-tuple-element.30), channel_id=1, source_target_pairs={{0,8},{8,16},{16,24},{1,9},{9,17},{17,25},{2,10},{10,18},{18,26},{... | collective-permute-start | bytes 172040 | tf_op jit(solution)/shard_map/ppermute | solution.py:23
  22.6 3.1 %collective-permute-start.6 = (f32[4,1,1792]{2,1,0:T(1,128)S(1)}, f32[4,1,1792]{2,1,0:T(1,128)S(1)}, u32[]{:S(2)}, u32[]{:S(2)}) collective-permute-start(f32[4,1,1792]{2,1,0:T(1,128)S(1)} %get-tuple-element.32), channel_id=1, source_target_pairs={{1,0},{2,1},{3,2},{4,3},{5,4},{6,5},{7,6},{0,7},{9,8},{10,9},{11,1... | collective-permute-start | bytes 86024 | tf_op jit(solution)/shard_map/ppermute | solution.py:26
  26.0 1.2 collective-permute-done.6
  27.2 3.5 %collective-permute-done.7 = f32[4,1,1792]{2,1,0:T(1,128)S(1)} collective-permute-done((f32[4,1,1792]{2,1,0:T(1,128)S(1)}, f32[4,1,1792]{2,1,0:T(1,128)S(1)}, u32[]{:S(2)}, u32[]{:S(2)}) %collective-permute-start.7) | collective-permute-done | bytes 28704 | tf_op jit(solution)/shard_map/ppermute | solution.py:23
  32.1 36.6 %all-gather = f32[32,4,64]{2,1,0:T(4,128)S(1)} all-gather(f32[1,4,64]{2,1,0:T(4,128)S(1)} %convolution_bitcast_fusion.5), channel_id=1, replica_groups=mesh['lat'=4,'lon'=8] {'lat','lon'}, dimensions={0}, use_global_device_ids=true | all-gather | bytes 33792 | tf_op jit(solution)/shard_map/all_gather | solution.py:119
  70.0 11.7 %cholesky.59 = f32[128,128]{1,0:T(8,128)S(1)} custom-call(f32[128,128]{1,0:T(8,128)S(1)} %fusion.33), custom_call_target="Cholesky" | custom-call | tf_op jit(solution)/shard_map/jit(cholesky)/cholesky | solution.py:69
  83.1 9.8 %custom-call.9 = f32[1,128,128]{1,2,0:T(8,128)S(1)} custom-call(f32[1,128,128]{2,1,0:T(8,128)S(1)} %fusion.8), custom_call_target="InvertDiagBlocksLowerTriangular" | custom-call | tf_op jit(solution)/shard_map/jit(_cho_solve)/triangular_solve | solution.py:71
  93.9 0.8 convolution_multiply_fusion.2
  94.8 0.7 fusion.205
  96.7 38.7 %all-gather.1 = f32[32,4,64]{2,1,0:T(4,128)S(1)} all-gather(f32[1,4,64]{2,1,0:T(4,128)S(1)} %convolution_bitcast_fusion.4), channel_id=1, replica_groups=mesh['lat'=4,'lon'=8] {'lat','lon'}, dimensions={0}, use_global_device_ids=true | all-gather | bytes 33792 | tf_op jit(solution)/shard_map/all_gather | solution.py:119
  136.7 11.7 %cholesky.70 = f32[128,128]{1,0:T(8,128)S(1)} custom-call(f32[128,128]{1,0:T(8,128)S(1)} %fusion.25), custom_call_target="Cholesky" | custom-call | tf_op jit(solution)/shard_map/jit(cholesky)/cholesky | solution.py:69
  149.8 9.8 %custom-call.10 = f32[1,128,128]{1,2,0:T(8,128)S(1)} custom-call(f32[1,128,128]{2,1,0:T(8,128)S(1)} %fusion.9), custom_call_target="InvertDiagBlocksLowerTriangular" | custom-call | tf_op jit(solution)/shard_map/jit(_cho_solve)/triangular_solve | solution.py:71
  162.7 37.1 %all-gather.2 = f32[32,4,64]{2,1,0:T(4,128)S(1)} all-gather(f32[1,4,64]{2,1,0:T(4,128)S(1)} %convolution_bitcast_fusion.3), channel_id=1, replica_groups=mesh['lat'=4,'lon'=8] {'lat','lon'}, dimensions={0}, use_global_device_ids=true | all-gather | bytes 33792 | tf_op jit(solution)/shard_map/all_gather | solution.py:119
  201.1 11.7 %cholesky.81 = f32[128,128]{1,0:T(8,128)S(1)} custom-call(f32[128,128]{1,0:T(8,128)S(1)} %fusion.17), custom_call_target="Cholesky" | custom-call | tf_op jit(solution)/shard_map/jit(cholesky)/cholesky | solution.py:69
  214.2 9.8 %custom-call.11 = f32[1,128,128]{1,2,0:T(8,128)S(1)} custom-call(f32[1,128,128]{2,1,0:T(8,128)S(1)} %fusion.10), custom_call_target="InvertDiagBlocksLowerTriangular" | custom-call | tf_op jit(solution)/shard_map/jit(_cho_solve)/triangular_solve | solution.py:71
  226.2 0.9 reshape.466
  (123 shorter events, 19.9 us)
Async XLA Ops:
  0.0 7.8 %copy-start = (f32[4,8,1792]{2,1,0:T(8,128)S(1)}, f32[4,8,1792]{2,1,0:T(8,128)}, u32[]{:S(2)}) copy-start(f32[4,8,1792]{2,1,0:T(8,128)} %param.18) | copy-start | bytes 688132
  0.9 15.1 %collective-permute-start = (f32[1,8,1792]{2,1,0:T(8,128)S(1)}, f32[1,8,1792]{2,1,0:T(8,128)S(1)}, u32[]{:S(2)}, u32[]{:S(2)}) collective-permute-start(f32[1,8,1792]{2,1,0:T(8,128)S(1)} %get-tuple-element.35), channel_id=1, source_target_pairs={{8,0},{16,8},{24,16},{9,1},{17,9},{25,17},{10,2},{18,10},{26,18},{... | collective-permute-start | bytes 172040 | tf_op jit(solution)/shard_map/ppermute | solution.py:26
  2.2 10.5 %copy-start.1 = (f32[3,128,64]{1,2,0:T(8,128)S(1)}, f32[3,128,64]{1,2,0:T(8,128)}, u32[]{:S(2)}) copy-start(f32[3,128,64]{1,2,0:T(8,128)} %param.28) | copy-start | bytes 294916
  2.2 13.8 %collective-permute-start.1 = (f32[1,8,1792]{2,1,0:T(8,128)S(1)}, f32[1,8,1792]{2,1,0:T(8,128)S(1)}, u32[]{:S(2)}, u32[]{:S(2)}) collective-permute-start(f32[1,8,1792]{2,1,0:T(8,128)S(1)} %get-tuple-element.34), channel_id=1, source_target_pairs={{0,8},{8,16},{16,24},{1,9},{9,17},{17,25},{2,10},{10,18},{18,26},{... | collective-permute-start | bytes 172040 | tf_op jit(solution)/shard_map/ppermute | solution.py:23
  7.9 3.1 %copy-start.6 = (f32[3,128]{1,0:T(4,128)S(1)}, f32[3,128]{1,0:T(4,128)}, u32[]{:S(2)}) copy-start(f32[3,128]{1,0:T(4,128)} %param.27) | copy-start | bytes 4612
  7.9 7.3 %collective-permute-start.2 = (f32[4,1,1792]{2,1,0:T(1,128)S(1)}, f32[4,1,1792]{2,1,0:T(1,128)S(1)}, u32[]{:S(2)}, u32[]{:S(2)}) collective-permute-start(f32[4,1,1792]{2,1,0:T(1,128)S(1)} %get-tuple-element.36), channel_id=1, source_target_pairs={{1,0},{2,1},{3,2},{4,3},{5,4},{6,5},{7,6},{0,7},{9,8},{10,9},{11,1... | collective-permute-start | bytes 86024 | tf_op jit(solution)/shard_map/ppermute | solution.py:26
  11.0 5.1 %collective-permute-start.3 = (f32[4,1,1792]{2,1,0:T(1,128)S(1)}, f32[4,1,1792]{2,1,0:T(1,128)S(1)}, u32[]{:S(2)}, u32[]{:S(2)}) collective-permute-start(f32[4,1,1792]{2,1,0:T(1,128)S(1)} %get-tuple-element.37), channel_id=1, source_target_pairs={{0,1},{1,2},{2,3},{3,4},{4,5},{5,6},{6,7},{7,0},{8,9},{9,10},{10,1... | collective-permute-start | bytes 86024 | tf_op jit(solution)/shard_map/ppermute | solution.py:23
  11.0 0.7 copy-start.7
  11.7 0.7 copy-start.2
  12.7 0.7 copy-start.8
  13.4 0.7 copy-start.9
  14.1 0.7 copy-start.10
  15.1 1.0 copy-start.5
  15.1 0.9 copy-start.3
  15.2 0.9 copy-start.4
  16.3 14.4 %collective-permute-start.4 = (f32[1,8,1792]{2,1,0:T(8,128)S(1)}, f32[1,8,1792]{2,1,0:T(8,128)S(1)}, u32[]{:S(2)}, u32[]{:S(2)}) collective-permute-start(f32[1,8,1792]{2,1,0:T(8,128)S(1)} %get-tuple-element.31), channel_id=1, source_target_pairs={{8,0},{16,8},{24,16},{9,1},{17,9},{25,17},{10,2},{18,10},{26,18},{... | collective-permute-start | bytes 172040 | tf_op jit(solution)/shard_map/ppermute | solution.py:26
  17.6 13.1 %collective-permute-start.5 = (f32[1,8,1792]{2,1,0:T(8,128)S(1)}, f32[1,8,1792]{2,1,0:T(8,128)S(1)}, u32[]{:S(2)}, u32[]{:S(2)}) collective-permute-start(f32[1,8,1792]{2,1,0:T(8,128)S(1)} %get-tuple-element.30), channel_id=1, source_target_pairs={{0,8},{8,16},{16,24},{1,9},{9,17},{17,25},{2,10},{10,18},{18,26},{... | collective-permute-start | bytes 172040 | tf_op jit(solution)/shard_map/ppermute | solution.py:23
  22.6 4.6 %collective-permute-start.6 = (f32[4,1,1792]{2,1,0:T(1,128)S(1)}, f32[4,1,1792]{2,1,0:T(1,128)S(1)}, u32[]{:S(2)}, u32[]{:S(2)}) collective-permute-start(f32[4,1,1792]{2,1,0:T(1,128)S(1)} %get-tuple-element.32), channel_id=1, source_target_pairs={{1,0},{2,1},{3,2},{4,3},{5,4},{6,5},{7,6},{0,7},{9,8},{10,9},{11,1... | collective-permute-start | bytes 86024 | tf_op jit(solution)/shard_map/ppermute | solution.py:26
  25.7 5.1 %collective-permute-start.7 = (f32[4,1,1792]{2,1,0:T(1,128)S(1)}, f32[4,1,1792]{2,1,0:T(1,128)S(1)}, u32[]{:S(2)}, u32[]{:S(2)}) collective-permute-start(f32[4,1,1792]{2,1,0:T(1,128)S(1)} %get-tuple-element.33), channel_id=1, source_target_pairs={{0,1},{1,2},{2,3},{3,4},{4,5},{5,6},{6,7},{7,0},{8,9},{9,10},{10,1... | collective-permute-start | bytes 86024 | tf_op jit(solution)/shard_map/ppermute | solution.py:23
where the time goes:
time: 227 us
  blocking collectives  112 us (49%)
  other arithmetic  70.6 us (31%)
  starting transfers between devices  19.3 us (9%)
  local copies, waits for them, and re-layouts  11.2 us (5%)
  matrix products  7.25 us (3%)
  waiting for transfers between devices  5.65 us (2%)
    all_gather x3, blocking collectives, body(): gathered = lax.all_gather(packed, ('lat', 'lon'), axis=0, tiled=True)  112 us
    another operation x9, other arithmetic, whiten(): factor = jnp.linalg.cholesky(cov)  37.2 us
    another operation x6, other arithmetic, whiten(): return (anom, jax.scipy.linalg.cho_solve((factor, True), rhs))  31.4 us
    ppermute x4, starting transfers between devices, with_halo(): lax.ppermute(lax.slice_in_dim(block, block.shape[dim] - width, None, axis...  10.5 us
    ppermute x4, starting transfers between devices, with_halo(): lax.ppermute(lax.slice_in_dim(block, 0, width, axis=dim), axis, backward)  8.72 us
  transfers between devices with their start and end apart: 8, of which 3 were waited for; matrix products, arithmetic and copies ran while one was open for 0% of the time, Pallas kernels for 0%

commit v1 on v0

v1 whole, which is shorter than its diff:
```python
import functools

import jax
import jax.numpy as jnp
from jax import lax
from jax.experimental import pallas as pl
from jax.experimental.pallas import tpu as pltpu
from jax.sharding import PartitionSpec as P

LEV = 28
MEMBERS = 64
SECTIONS = 2
BATCH_GROUPS = 3
CAP = 4
LANES = 128
PIVOTS = 4

advect_coef = 0.2
MESH = pl.DeviceIdType.MESH
HIGHEST = lax.Precision.HIGHEST
SLOT_ROWS = -(-(BATCH_GROUPS * CAP) // 16) * 8


def floor_div(value, divisor):
    return jnp.floor((value + 0.5) * (1.0 / divisor))


def dot_t(a, b, precision=None):
    return lax.dot_general(
        a, b, (((1,), (1,)), ((), ())), precision=precision, preferred_element_type=jnp.float32
    )


def dot_n(a, b, precision=None):
    return lax.dot_general(
        a, b, (((1,), (0,)), ((), ())), precision=precision, preferred_element_type=jnp.float32
    )


def split(value):
    high = value.astype(jnp.bfloat16)
    low = (value - high.astype(jnp.float32)).astype(jnp.bfloat16)
    return high, low


def iota(shape, dim):
    return lax.broadcasted_iota(jnp.int32, shape, dim)


def column(row):
    n = row.shape[1]
    return jnp.sum(
        jnp.where(iota((n, n), 0) == iota((n, n), 1), row, 0.0), axis=1, keepdims=True
    )


def forecast_kernel(
    lat_n,
    lon_n,
    ens_ref,
    north_ref,
    east_ref,
    spread_ref,
    owner_ref,
    site_ref,
    state_ref,
    gather_ref,
    rank_ref,
    mid,
    edge,
    halo_lat,
    halo_lon,
    slots,
    send_sem,
    recv_sem,
    lon_send,
    lon_recv,
    lat_send,
    lat_recv,
):
    ilat = lax.axis_index("lat")
    ilon = lax.axis_index("lon")
    tile_lat, tile_lon, width = ens_ref.shape
    pairs = width // LANES
    lon_peers = [lax.rem(ilon + d, lon_n) for d in range(1, lon_n)]
    lat_peers = [lax.rem(ilat + d, lat_n) for d in range(1, lat_n)]

    barrier = pltpu.get_barrier_semaphore()
    for peer in lon_peers:
        pl.semaphore_signal(barrier, inc=1, device_id=(ilat, peer), device_id_type=MESH)
    for peer in lat_peers:
        pl.semaphore_signal(barrier, inc=1, device_id=(peer, ilon), device_id_type=MESH)

    def fill_edges(section, src):
        for i in range(tile_lat):
            edge[section, 0, i : i + 1, :] = src[i, tile_lon - 1 : tile_lon, :]
            edge[section, 1, i : i + 1, :] = src[i, 0:1, :]

    def start(section, src):
        up = lax.rem(ilat + 1, lat_n)
        down = lax.rem(ilat + lat_n - 1, lat_n)
        right = lax.rem(ilon + 1, lon_n)
        left = lax.rem(ilon + lon_n - 1, lon_n)
        moves = (
            (src.at[tile_lat - 1], halo_lat.at[section, 0], (up, ilon)),
            (src.at[0], halo_lat.at[section, 1], (down, ilon)),
            (edge.at[section, 0], halo_lon.at[section, 0], (ilat, right)),
            (edge.at[section, 1], halo_lon.at[section, 1], (ilat, left)),
        )
        copies = []
        for n, (a, b, device) in enumerate(moves):
            copy = pltpu.make_async_remote_copy(
                src_ref=a,
                dst_ref=b,
                send_sem=send_sem.at[section, n],
                recv_sem=recv_sem.at[section, n],
                device_id=device,
                device_id_type=MESH,
            )
            copy.start()
            copies.append(copy)
        return copies

    fill_edges(0, ens_ref)
    pl.semaphore_wait(barrier, len(lon_peers) + len(lat_peers))
    copies = start(0, ens_ref)

    same = iota((tile_lon, tile_lon), 0) == iota((tile_lon, tile_lon), 1)
    coef = []
    for i in range(tile_lat):
        s, n, e = (
            jnp.sum(jnp.where(same, ref[i : i + 1, :], 0.0), axis=1, keepdims=True)
            for ref in (spread_ref, north_ref, east_ref)
        )
        n = advect_coef * n
        e = advect_coef * e
        coef.append((1.0 - 4.0 * s, s - n, s + n, s - e, s + e))

    count = owner_ref.shape[1]
    me = (ilat * lon_n + ilon).astype(jnp.float32)
    half = SLOT_ROWS
    slot_iota = iota((2 * half, count), 0)
    slot_id = (2 * (slot_iota % half) + slot_iota // half).astype(jnp.float32)
    slot_row = jnp.zeros((2 * half, 1), jnp.float32)
    slot_odd = jnp.zeros((2 * half, 1), jnp.float32)
    rank_ref[...] = jnp.zeros(rank_ref.shape, jnp.float32)
    for k in range(BATCH_GROUPS):
        owner = owner_ref[k : k + 1, :].astype(jnp.float32)
        site = site_ref[k : k + 1, :].astype(jnp.float32)
        before = iota((count, count), 0) < iota((count, count), 1)
        earlier = (column(owner) == owner) & before
        rank = jnp.sum(jnp.where(earlier, 1.0, 0.0), axis=0, keepdims=True)
        rank_ref[k : k + 1, :] = rank
        cell = floor_div(site, LEV)
        level = site - LEV * cell
        cell_lat = floor_div(cell, tile_lon)
        cell_lon = cell - tile_lon * cell_lat
        pair = floor_div(level, 2)
        row = (cell_lat * pairs + pair) * tile_lon + cell_lon
        mine = (owner == me) & (slot_id == rank + float(CAP * k))
        slot_row += jnp.sum(jnp.where(mine, row, 0.0), axis=1, keepdims=True)
        slot_odd += jnp.sum(jnp.where(mine, level - 2.0 * pair, 0.0), axis=1, keepdims=True)
    rows = tile_lat * width // LANES * tile_lon
    pick = jnp.where(
        iota((2 * half, rows), 1).astype(jnp.float32) == slot_row, 1.0, 0.0
    )

    src = ens_ref
    for section in range(SECTIONS):
        for copy in copies:
            copy.wait()
        last = section == SECTIONS - 1
        for i in range(tile_lat):
            centre, c_n, c_s, c_e, c_w = coef[i]
            here = src[i]
            if i + 1 < tile_lat:
                above = src[i + 1]
            else:
                above = jnp.where(ilat == lat_n - 1, 0.0, halo_lat[section, 1])
            if i > 0:
                below = src[i - 1]
            else:
                below = jnp.where(ilat == 0, 0.0, halo_lat[section, 0])
            east = jnp.concatenate([here[1:], halo_lon[section, 1, i : i + 1, :]], axis=0)
            west = jnp.concatenate([halo_lon[section, 0, i : i + 1, :], here[:-1]], axis=0)
            new = centre * here + c_n * above + c_s * below + c_e * east + c_w * west
            if last:
                for p in range(pairs):
                    at = (i * pairs + p) * tile_lon
                    state_ref[at : at + tile_lon, :] = new[:, p * LANES : (p + 1) * LANES]
            else:
                mid[section, i] = new
        if not last:
            src = mid.at[section]
            fill_edges(section + 1, src)
            copies = start(section + 1, src)

    taken = dot_n(pick, state_ref[...], HIGHEST)
    first, second = taken[:half], taken[half:]
    first = jnp.where(slot_odd[:half] < 0.5, first, pltpu.roll(first, MEMBERS, 1))
    second = jnp.where(slot_odd[half:] > 0.5, second, pltpu.roll(second, MEMBERS, 1))
    low_half = iota((half, LANES), 1) < MEMBERS
    slots[ilat, ilon] = jnp.where(low_half, first, second)

    def share(src_at, peers, sends, recvs, device_of):
        out = []
        for n, peer in enumerate(peers):
            copy = pltpu.make_async_remote_copy(
                src_ref=src_at,
                dst_ref=src_at,
                send_sem=sends.at[n],
                recv_sem=recvs.at[n],
                device_id=device_of(peer),
                device_id_type=MESH,
            )
            copy.start()
            out.append(copy)
        for copy in out:
            copy.wait()

    share(slots.at[ilat, ilon], lon_peers, lon_send, lon_recv, lambda peer: (ilat, peer))
    share(slots.at[ilat], lat_peers, lat_send, lat_recv, lambda peer: (peer, ilon))
    gather_ref[...] = slots[...].reshape(gather_ref.shape)


def taper(dist, inverse_radius):
    z = dist * inverse_radius
    inner = 1.0 + z * z * (-5.0 / 3.0 + z * (0.625 + z * (0.5 - 0.25 * z)))
    o = jnp.maximum(z, 1.0)
    outer = (
        4.0
        + o * (-5.0 + o * (5.0 / 3.0 + o * (0.625 + o * (-0.5 + o * (1.0 / 12.0)))))
        - (2.0 / 3.0) / o
    )
    return jnp.where(z <= 1.0, inner, jnp.where(z < 2.0, outer, 0.0))


def gauss_jordan(aug):
    size = aug.shape[0]
    blocks = [aug[i : i + 8] for i in range(0, size, 8)]
    sub = iota((8, LANES), 0)
    for base in range(0, size, PIVOTS):
        home, at = base // 8, base % 8
        cols = [
            [jnp.broadcast_to(block[:, base + j : base + j + 1], (8, LANES)) for block in blocks]
            for j in range(PIVOTS)
        ]
        rows = [blocks[home][at + i : at + i + 1] for i in range(PIVOTS)]
        c = [[cols[j][home][at + i : at + i + 1] for j in range(PIVOTS)] for i in range(PIVOTS)]
        for i in range(PIVOTS):
            inverse = 1.0 / c[i][i]
            rows[i] = rows[i] * inverse
            for j in range(i + 1, PIVOTS):
                c[i][j] = c[i][j] * inverse
            for r in range(PIVOTS):
                if r != i:
                    f = c[r][i]
                    rows[r] = rows[r] - f * rows[i]
                    for j in range(i + 1, PIVOTS):
                        c[r][j] = c[r][j] - f * c[i][j]
        wide = [jnp.broadcast_to(row, (8, LANES)) for row in rows]
        for b in range(len(blocks)):
            new = blocks[b]
            for j in range(PIVOTS):
                new = new - cols[j][b] * wide[j]
            if b == home:
                for j in range(PIVOTS):
                    new = jnp.where(sub == at + j, wide[j], new)
            blocks[b] = new
    return jnp.concatenate(blocks, axis=0)


def update_kernel(
    lat_n,
    lon_n,
    state_ref,
    gather_ref,
    rank_ref,
    owner_ref,
    site_ref,
    class_ref,
    cutoff_ref,
    value_ref,
    var_ref,
    noise_ref,
    out_ref,
    x_ref,
    noise_wide,
):
    tile_lat, tile_lon, width = out_ref.shape
    pairs = width // LANES
    ilat = lax.axis_index("lat")
    ilon = lax.axis_index("lon")
    lon_cells = float(tile_lon * lon_n)
    count = owner_ref.shape[1]
    scale = 1.0 / (MEMBERS - 1)
    low_lanes = iota((count, LANES), 1) < MEMBERS

    rows_of = []
    stacked = []
    for k in range(BATCH_GROUPS):
        owner = owner_ref[k : k + 1, :].astype(jnp.float32)
        site = site_ref[k : k + 1, :].astype(jnp.float32)
        classes = class_ref[k : k + 1, :]
        cell = floor_div(site, LEV)
        cell_lat = floor_div(cell, tile_lon)
        tile_row = floor_div(owner, lon_n)
        glat = tile_row * tile_lat + cell_lat
        glon = (owner - lon_n * tile_row) * tile_lon + cell - tile_lon * cell_lat
        radius = jnp.zeros((1, count), jnp.float32)
        for c in range(cutoff_ref.shape[0]):
            radius = jnp.where(classes == c, cutoff_ref[c].astype(jnp.float32), radius)
        slot = rank_ref[k : k + 1, :] + float(CAP * k)
        slot_half = floor_div(slot, 2)
        rows_of.append((glat, glon, 1.0 / radius))
        stacked += [
            glat,
            glon,
            owner * SLOT_ROWS + slot_half,
            slot - 2.0 * slot_half,
            value_ref[k : k + 1, :],
            var_ref[k : k + 1, :],
            jnp.zeros((2, count), jnp.float32),
        ]
    table = jnp.concatenate(stacked, axis=0).T

    def col(k, n):
        return table[:, 8 * k + n : 8 * k + n + 1]

    def rho_of(lat_at, lon_at, k):
        glat, glon, inverse_radius = rows_of[k]
        dlat = jnp.abs(lat_at - glat)
        dlon = jnp.abs(lon_at - glon)
        dlon = jnp.minimum(dlon, lon_cells - dlon)
        return scale * taper(jnp.sqrt(dlat * dlat + dlon * dlon), inverse_radius)

    slots = gather_ref.shape[0]
    priors = []
    for k in range(BATCH_GROUPS):
        pick = jnp.where(iota((count, slots), 1).astype(jnp.float32) == col(k, 2), 1.0, 0.0)
        taken = dot_n(pick, gather_ref[...], HIGHEST)
        turned = pltpu.roll(taken, MEMBERS, 1)
        odd = col(k, 3) > 0.5
        priors.append(jnp.where(odd != low_lanes, taken, turned))

    for k in range(BATCH_GROUPS):
        prior = priors[k]
        var = col(k, 5)
        inverse_var = 1.0 / var
        anom = prior - jnp.mean(prior, axis=1, keepdims=True)
        noise_wide[:, :MEMBERS] = noise_ref[k]
        noise_wide[:, MEMBERS:] = noise_ref[k]
        rhs = col(k, 4) + jnp.sqrt(var) * noise_wide[...] - prior
        both = inverse_var * jnp.where(low_lanes, anom, rhs)
        aug = scale * dot_n(anom.T[:MEMBERS], both, HIGHEST)
        aug += jnp.where(iota(aug.shape, 0) == iota(aug.shape, 1), 1.0, 0.0)
        solved = gauss_jordan(aug)
        solved = jnp.where(
            iota(solved.shape, 1) < MEMBERS, pltpu.roll(solved, MEMBERS, 1), solved
        )
        white = inverse_var * (rhs - dot_n(anom[:, :MEMBERS], solved, HIGHEST))

        for later in range(k + 1, BATCH_GROUPS):
            cov = dot_t(priors[later][:, :MEMBERS], anom[:, :MEMBERS], HIGHEST)
            cov = cov * rho_of(col(later, 0), col(later, 1), k)
            priors[later] = priors[later] + dot_n(cov, white, HIGHEST)

        wide_anom = jnp.concatenate(
            [jnp.where(low_lanes, anom, 0.0), jnp.where(low_lanes, 0.0, anom)], axis=0
        )
        wide_white = jnp.concatenate(
            [jnp.where(low_lanes, white, 0.0), jnp.where(low_lanes, 0.0, white)], axis=0
        )
        rho = []
        for i in range(tile_lat):
            lat_at = (ilat * tile_lat + i).astype(jnp.float32)
            lon_at = (ilon * tile_lon + iota((tile_lon, 1), 0)).astype(jnp.float32)
            one = rho_of(lat_at, lon_at, k)
            rho.append(jnp.concatenate([one, one], axis=1)[None])
        rho = jnp.stack(rho, axis=0)

        x = state_ref[...] if k == 0 else x_ref[...]
        x_high, x_low = split(x)
        a_high, a_low = split(wide_anom)
        cov = dot_t(
            jnp.concatenate([x_high, x_low], axis=1), jnp.concatenate([a_high, a_high], axis=1)
        ) + dot_t(x_high, a_low)
        cov = cov.reshape(tile_lat, pairs, tile_lon, 2 * count) * rho
        cov = cov.reshape(tile_lat * pairs * tile_lon, 2 * count)
        c_high, c_low = split(cov)
        w_high, w_low = split(wide_white)
        two = dot_n(c_high, jnp.concatenate([w_high, w_low], axis=1))
        new = x + (two[:, :LANES] + two[:, LANES:] + dot_n(c_low, w_high))
        if k + 1 < BATCH_GROUPS:
            x_ref[...] = new
        else:
            for i in range(tile_lat):
                for p in range(pairs):
                    at = (i * pairs + p) * tile_lon
                    out_ref[i, :, p * LANES : (p + 1) * LANES] = new[at : at + tile_lon]


def body(
    ensemble,
    northward_wind,
    eastward_wind,
    spreading_strength,
    measurement_home_subdomain,
    obs_site,
    obs_class,
    cutoff_table,
    obs_value,
    obs_var,
    obs_noise,
):
    lat_n = lax.axis_size("lat")
    lon_n = lax.axis_size("lon")
    tile_lat, tile_lon, width = ensemble.shape
    rows = tile_lat * tile_lon * width // LANES
    count = obs_site.shape[1]
    vmem = pl.BlockSpec(memory_space=pltpu.VMEM)
    smem = pl.BlockSpec(memory_space=pltpu.SMEM)
    f32 = jnp.float32
    dma = pltpu.SemaphoreType.DMA
    state, gathered, rank = pl.pallas_call(
        functools.partial(forecast_kernel, lat_n, lon_n),
        out_shape=(
            jax.ShapeDtypeStruct((rows, LANES), f32),
            jax.ShapeDtypeStruct((lat_n * lon_n * SLOT_ROWS, LANES), f32),
            jax.ShapeDtypeStruct((8, count), f32),
        ),
        in_specs=[vmem] * 6,
        out_specs=(vmem, vmem, vmem),
        scratch_shapes=[
            pltpu.VMEM((SECTIONS - 1, tile_lat, tile_lon, width), f32),
            pltpu.VMEM((SECTIONS, 2, tile_lat, width), f32),
            pltpu.VMEM((SECTIONS, 2, tile_lon, width), f32),
            pltpu.VMEM((SECTIONS, 2, tile_lat, width), f32),
            pltpu.VMEM((lat_n, lon_n, SLOT_ROWS, LANES), f32),
            dma((SECTIONS, 4)),
            dma((SECTIONS, 4)),
            dma((lon_n - 1,)),
            dma((lon_n - 1,)),
            dma((lat_n - 1,)),
            dma((lat_n - 1,)),
        ],
        compiler_params=pltpu.CompilerParams(
            collective_id=0, has_side_effects=True, vmem_limit_bytes=32 << 20
        ),
    )(
        ensemble,
        northward_wind,
        eastward_wind,
        spreading_strength,
        measurement_home_subdomain,
        obs_site,
    )
    return pl.pallas_call(
        functools.partial(update_kernel, lat_n, lon_n),
        out_shape=jax.ShapeDtypeStruct(ensemble.shape, f32),
        in_specs=[vmem] * 6 + [smem] + [vmem] * 3,
        out_specs=vmem,
        scratch_shapes=[pltpu.VMEM((rows, LANES), f32), pltpu.VMEM((count, LANES), f32)],
        compiler_params=pltpu.CompilerParams(vmem_limit_bytes=48 << 20),
    )(
        state,
        gathered,
        rank,
        measurement_home_subdomain,
        obs_site,
        obs_class,
        cutoff_table,
        obs_value,
        obs_var,
        obs_noise,
    )


def solution(mesh):
    placed = (
        P("lat", "lon", None),
        P("lat", "lon"),
        P("lat", "lon"),
        P("lat", "lon"),
        P(),
        P(),
        P(),
        P(),
        P(),
        P(),
        P(),
    )
    return jax.shard_map(
        body, mesh=mesh, in_specs=placed, out_specs=P("lat", "lon", None), check_vma=False
    )
```

time: 227 us -> 36.7 us (0.16)
  blocking collectives: 112 us -> 0 us
  other arithmetic: 70.6 us -> 0 us
  Pallas kernels: 0 us -> 34.6 us
  starting transfers between devices: 19.3 us -> 0 us
  local copies, waits for them, and re-layouts: 11.2 us -> 1.8 us
  matrix products: 7.25 us -> 0 us
  waiting for transfers between devices: 5.65 us -> 0 us
    all_gather x3 -> x0, blocking collectives: 112 us -> none  [body(): gathered = lax.all_gather(packed, ('lat', 'lon'), axis=0, tiled=True)]
    another operation x15 -> x0, other arithmetic: 68.6 us -> none  [the longest x9 37.2 us: whiten(): factor = jnp.linalg.cholesky(cov)]
    pallas_call x0 -> x2, Pallas kernels: none -> 34.6 us  [the longest x1 21.7 us: body(): pl.pallas_call(functools.partial(forecast_kernel, lat_n, lon_n), out_shap...]
    ppermute x8 -> x0, starting transfers between devices: 19.3 us -> none  [the longest x4 10.5 us: with_halo(): lax.ppermute(lax.slice_in_dim(block, block.shape[dim] - width, None, axis...]
    ppermute x8 -> x0, waiting for transfers between devices: 5.65 us -> none  [the longest x4 4.39 us: with_halo(): lax.ppermute(lax.slice_in_dim(block, block.shape[dim] - width, None, axis...]
    dot_general x12 -> x0, matrix products: 5.45 us -> none  [the longest x3 2.04 us: body(): jnp.einsum('clm,jm->clj', xp, part_anom, precision=lax.Precision.HIGHEST)]
    gather x6 -> x0, local copies, waits for them, and re-layouts: 3.87 us -> none  [the longest x3 1.94 us: body(): picked = jnp.take(flat, site, axis=0)]
  transfers between devices with their start and end apart: 8 -> 0, of which waited for: 3 -> 0; matrix products, arithmetic and copies ran while one was open for 0% -> 0% of each run, Pallas kernels for 0% -> 0%
where the time goes in v1:
time: 36.7 us; the launch traced here: 36.5 us
  Pallas kernels  34.6 us (94%)
  local copies, waits for them, and re-layouts  1.8 us (5%)
    pallas_call x1, Pallas kernels, body(): pl.pallas_call(functools.partial(forecast_kernel, lat_n, lon_n), out_shap...  21.7 us
    pallas_call x1, Pallas kernels, body(): pl.pallas_call(functools.partial(update_kernel, lat_n, lon_n), out_shape=...  12.9 us
    unnamed x21, local copies, waits for them, and re-layouts  1.8 us

profile of v1, /device:TPU:0, one launch (start us, length us, event | category | flops | bytes accessed | tf_op | source)
XLA Modules:
  0.0 36.5 jit_solution(17335519106714379157)
XLA Ops:
  0.0 0.0 copy-start.2
  0.0 0.0 copy-start.1
  0.0 0.0 copy-start.5
  0.0 0.0 copy-start.4
  0.0 0.0 copy-start.3
  0.0 0.0 copy-start
  0.0 1.1 %copy.12.noise_ref = f32[3,128,64]{2,1,0:T(8,128)S(1)} copy(f32[3,128,64]{1,2,0:T(8,128)} %param.21) | data formatting | bytes 196608 | tf_op args[10]
  1.1 0.0 copy-done.2
  1.1 0.0 copy-done.1
  1.1 0.0 copy-done.5
  1.2 0.0 copy-done.4
  1.2 0.0 copy-done.3
  1.2 0.0 copy-done
  1.2 0.0 copy-start.8
  1.2 21.7 %shard_map.109 = (f32[448,128]{1,0:T(8,128)S(1)}, f32[256,128]{1,0:T(8,128)S(1)}, f32[8,128]{1,0:T(8,128)S(1)}) custom-call(f32[4,8,1792]{2,1,0:T(8,128)S(1)} %copy-done, f32[4,8]{1,0:T(4,128)S(1)} %copy-done.3, f32[4,8]{1,0:T(4,128)S(1)} %copy-done.4, f32[4,8]{1,0:T(4,128)S(1)} %copy-done.5, s32[3,128]{1,0:T(4,128)S(1)} %copy-done.1, s32[3,128]{1,0:T(4,128)S(1)} %copy-done.2), custom_call_target="tpu_custom_call" | custom-call | tf_op jit(solution)/shard_map/pallas_call | solution.py:425
  22.9 0.0 copy-start.7
  22.9 0.0 copy-start.6
  22.9 0.0 copy-start.9
  22.9 0.0 copy-done.8
  22.9 0.6 %copy-done.7 = f32[3,128]{1,0:T(4,128)S(1)} copy-done((f32[3,128]{1,0:T(4,128)S(1)}, f32[3,128]{1,0:T(4,128)}, u32[]{:S(2)}) %copy-start.7) | copy-done | bytes 1560
  23.6 0.0 copy-done.6
  23.6 0.0 copy-done.9
  23.6 12.9 %shard_map.110 = f32[4,8,1792]{2,1,0:T(8,128)} custom-call(f32[448,128]{1,0:T(8,128)S(1)} %get-tuple-element.8.state_ref, f32[256,128]{1,0:T(8,128)S(1)} %get-tuple-element.9.gather_ref, f32[8,128]{1,0:T(8,128)S(1)} %get-tuple-element.10.rank_ref, s32[3,128]{1,0:T(4,128)S(1)} %copy-done.1, s32[3,128]{1,0:T(4,128)S(1)} %copy-done.2, s32[3,128]{1,0:T(4,128)S(1)} %copy-done.6, ...), custom_call_target="tpu_custom_call" | custom-call | tf_op jit(solution)/shard_map/pallas_call | solution.py:458
Async XLA Ops:
  0.0 1.1 %copy-start.2 = (s32[3,128]{1,0:T(4,128)S(1)}, s32[3,128]{1,0:T(4,128)}, u32[]{:S(2)}) copy-start(s32[3,128]{1,0:T(4,128)} %site_ref.3) | copy-start | bytes 4612
  0.0 1.1 %copy-start.1 = (s32[3,128]{1,0:T(4,128)S(1)}, s32[3,128]{1,0:T(4,128)}, u32[]{:S(2)}) copy-start(s32[3,128]{1,0:T(4,128)} %owner_ref.3) | copy-start | bytes 4612
  0.0 1.1 %copy-start.5 = (f32[4,8]{1,0:T(4,128)S(1)}, f32[4,8]{1,0:T(4,128)}, u32[]{:S(2)}) copy-start(f32[4,8]{1,0:T(4,128)} %spread_ref.1) | copy-start | bytes 388
  0.0 1.2 %copy-start.4 = (f32[4,8]{1,0:T(4,128)S(1)}, f32[4,8]{1,0:T(4,128)}, u32[]{:S(2)}) copy-start(f32[4,8]{1,0:T(4,128)} %east_ref.1) | copy-start | bytes 388
  0.0 1.2 %copy-start.3 = (f32[4,8]{1,0:T(4,128)S(1)}, f32[4,8]{1,0:T(4,128)}, u32[]{:S(2)}) copy-start(f32[4,8]{1,0:T(4,128)} %north_ref.1) | copy-start | bytes 388
  0.0 1.2 %copy-start = (f32[4,8,1792]{2,1,0:T(8,128)S(1)}, f32[4,8,1792]{2,1,0:T(8,128)}, u32[]{:S(2)}) copy-start(f32[4,8,1792]{2,1,0:T(8,128)} %ens_ref.1) | copy-start | bytes 688132
  1.2 21.8 %copy-start.8 = (f32[3,128]{1,0:T(4,128)S(1)}, f32[3,128]{1,0:T(4,128)}, u32[]{:S(2)}) copy-start(f32[3,128]{1,0:T(4,128)} %var_ref.1) | copy-start | bytes 4612
  22.9 0.7 %copy-start.7 = (f32[3,128]{1,0:T(4,128)S(1)}, f32[3,128]{1,0:T(4,128)}, u32[]{:S(2)}) copy-start(f32[3,128]{1,0:T(4,128)} %value_ref.1) | copy-start | bytes 4612
  22.9 0.7 %copy-start.6 = (s32[3,128]{1,0:T(4,128)S(1)}, s32[3,128]{1,0:T(4,128)}, u32[]{:S(2)}) copy-start(s32[3,128]{1,0:T(4,128)} %class_ref.1) | copy-start | bytes 4612
  22.9 0.7 %copy-start.9 = (s32[8]{0:T(128)S(1)}, s32[8]{0:T(128)}, u32[]{:S(2)}) copy-start(s32[8]{0:T(128)} %cutoff_ref.1) | copy-start | bytes 100

commit v2 on v1

--- a/solution.py
+++ b/solution.py
@@ -17,7 +17,6 @@
 
 advect_coef = 0.2
 MESH = pl.DeviceIdType.MESH
-HIGHEST = lax.Precision.HIGHEST
 SLOT_ROWS = -(-(BATCH_GROUPS * CAP) // 16) * 8
 
 
@@ -25,15 +24,15 @@
     return jnp.floor((value + 0.5) * (1.0 / divisor))
 
 
-def dot_t(a, b, precision=None):
+def dot_t(a, b):
     return lax.dot_general(
-        a, b, (((1,), (1,)), ((), ())), precision=precision, preferred_element_type=jnp.float32
-    )
-
-
-def dot_n(a, b, precision=None):
+        a, b, (((1,), (1,)), ((), ())), preferred_element_type=jnp.float32
+    )
+
+
+def dot_n(a, b):
     return lax.dot_general(
-        a, b, (((1,), (0,)), ((), ())), precision=precision, preferred_element_type=jnp.float32
+        a, b, (((1,), (0,)), ((), ())), preferred_element_type=jnp.float32
     )
 
 
@@ -43,6 +42,18 @@
     return high, low
 
 
+def dot3(dot, a, b):
+    a_high, a_low = split(a)
+    b_high, b_low = split(b)
+    return dot(a_high, b_high) + (dot(a_high, b_low) + dot(a_low, b_high))
+
+
+def pick_rows(chosen, table):
+    high, low = split(table)
+    both = dot_n(chosen, jnp.concatenate([high, low], axis=1))
+    return both[:, : table.shape[1]] + both[:, table.shape[1] :]
+
+
 def iota(shape, dim):
     return lax.broadcasted_iota(jnp.int32, shape, dim)
 
@@ -57,15 +68,30 @@
 def forecast_kernel(
     lat_n,
     lon_n,
+    ens_hbm,
+    north_hbm,
+    east_hbm,
+    spread_hbm,
+    owner_hbm,
+    site_hbm,
+    class_hbm,
+    value_hbm,
+    var_hbm,
+    cutoff_hbm,
+    state_ref,
+    gather_ref,
+    meta_ref,
     ens_ref,
     north_ref,
     east_ref,
     spread_ref,
     owner_ref,
     site_ref,
-    state_ref,
-    gather_ref,
-    rank_ref,
+    class_ref,
+    value_ref,
+    var_ref,
+    cutoff_ref,
+    load_sem,
     mid,
     edge,
     halo_lat,
@@ -91,39 +117,66 @@
     for peer in lat_peers:
         pl.semaphore_signal(barrier, inc=1, device_id=(peer, ilon), device_id_type=MESH)
 
+    loads = []
+    for n, (a, b) in enumerate(
+        (
+            (ens_hbm, ens_ref),
+            (spread_hbm, spread_ref),
+            (north_hbm, north_ref),
+            (east_hbm, east_ref),
+            (owner_hbm, owner_ref),
+            (site_hbm, site_ref),
+            (class_hbm, class_ref),
+            (cutoff_hbm, cutoff_ref),
+            (value_hbm, value_ref),
+            (var_hbm, var_ref),
+        )
+    ):
+        load = pltpu.make_async_copy(a, b, load_sem.at[n])
+        load.start()
+        loads.append(load)
+
     def fill_edges(section, src):
         for i in range(tile_lat):
             edge[section, 0, i : i + 1, :] = src[i, tile_lon - 1 : tile_lon, :]
             edge[section, 1, i : i + 1, :] = src[i, 0:1, :]
 
-    def start(section, src):
-        up = lax.rem(ilat + 1, lat_n)
-        down = lax.rem(ilat + lat_n - 1, lat_n)
-        right = lax.rem(ilon + 1, lon_n)
-        left = lax.rem(ilon + lon_n - 1, lon_n)
-        moves = (
-            (src.at[tile_lat - 1], halo_lat.at[section, 0], (up, ilon)),
-            (src.at[0], halo_lat.at[section, 1], (down, ilon)),
-            (edge.at[section, 0], halo_lon.at[section, 0], (ilat, right)),
-            (edge.at[section, 1], halo_lon.at[section, 1], (ilat, left)),
-        )
-        copies = []
-        for n, (a, b, device) in enumerate(moves):
-            copy = pltpu.make_async_remote_copy(
-                src_ref=a,
-                dst_ref=b,
-                send_sem=send_sem.at[section, n],
-                recv_sem=recv_sem.at[section, n],
-                device_id=device,
-                device_id_type=MESH,
-            )
-            copy.start()
-            copies.append(copy)
-        return copies
-
+    up = lax.rem(ilat + 1, lat_n)
+    down = lax.rem(ilat + lat_n - 1, lat_n)
+    right = lax.rem(ilon + 1, lon_n)
+    left = lax.rem(ilon + lon_n - 1, lon_n)
+
+    def send(section, n, a, b, device):
+        copy = pltpu.make_async_remote_copy(
+            src_ref=a,
+            dst_ref=b,
+            send_sem=send_sem.at[section, n],
+            recv_sem=recv_sem.at[section, n],
+            device_id=device,
+            device_id_type=MESH,
+        )
+        copy.start()
+        return copy
+
+    def send_rows(section, src):
+        return [
+            send(section, 0, src.at[tile_lat - 1], halo_lat.at[section, 0], (up, ilon)),
+            send(section, 1, src.at[0], halo_lat.at[section, 1], (down, ilon)),
+        ]
+
+    def send_columns(section):
+        return [
+            send(section, 2, edge.at[section, 0], halo_lon.at[section, 0], (ilat, right)),
+            send(section, 3, edge.at[section, 1], halo_lon.at[section, 1], (ilat, left)),
+        ]
+
+    pl.semaphore_wait(barrier, len(lon_peers) + len(lat_peers))
+    copies = send_rows(0, ens_hbm)
+    loads[0].wait()
     fill_edges(0, ens_ref)
-    pl.semaphore_wait(barrier, len(lon_peers) + len(lat_peers))
-    copies = start(0, ens_ref)
+    copies += send_columns(0)
+    for load in loads[1:]:
+        load.wait()
 
     same = iota((tile_lon, tile_lon), 0) == iota((tile_lon, tile_lon), 1)
     coef = []
@@ -143,14 +196,12 @@
     slot_id = (2 * (slot_iota % half) + slot_iota // half).astype(jnp.float32)
     slot_row = jnp.zeros((2 * half, 1), jnp.float32)
     slot_odd = jnp.zeros((2 * half, 1), jnp.float32)
-    rank_ref[...] = jnp.zeros(rank_ref.shape, jnp.float32)
     for k in range(BATCH_GROUPS):
         owner = owner_ref[k : k + 1, :].astype(jnp.float32)
         site = site_ref[k : k + 1, :].astype(jnp.float32)
         before = iota((count, count), 0) < iota((count, count), 1)
         earlier = (column(owner) == owner) & before
         rank = jnp.sum(jnp.where(earlier, 1.0, 0.0), axis=0, keepdims=True)
-        rank_ref[k : k + 1, :] = rank
         cell = floor_div(site, LEV)
         level = site - LEV * cell
         cell_lat = floor_div(cell, tile_lon)
@@ -160,10 +211,29 @@
         mine = (owner == me) & (slot_id == rank + float(CAP * k))
         slot_row += jnp.sum(jnp.where(mine, row, 0.0), axis=1, keepdims=True)
         slot_odd += jnp.sum(jnp.where(mine, level - 2.0 * pair, 0.0), axis=1, keepdims=True)
+        tile_row = floor_div(owner, lon_n)
+        radius = jnp.zeros((1, count), jnp.float32)
+        for c in range(cutoff_ref.shape[0]):
+            radius = jnp.where(
+                class_ref[k : k + 1, :] == c, cutoff_ref[c].astype(jnp.float32), radius
+            )
+        slot = rank + float(CAP * k)
+        slot_half = floor_div(slot, 2)
+        meta = (
+            tile_row * tile_lat + cell_lat,
+            (owner - lon_n * tile_row) * tile_lon + cell_lon,
+            owner * SLOT_ROWS + slot_half,
+            slot - 2.0 * slot_half,
+            value_ref[k : k + 1, :],
+            var_ref[k : k + 1, :],
+            1.0 / radius,
+            jnp.zeros((1, count), jnp.float32),
+        )
+        meta_ref[8 * k : 8 * k + 8, :] = jnp.concatenate(meta, axis=0)
     rows = tile_lat * width // LANES * tile_lon
     pick = jnp.where(
         iota((2 * half, rows), 1).astype(jnp.float32) == slot_row, 1.0, 0.0
-    )
+    ).astype(jnp.bfloat16)
 
     src = ens_ref
     for section in range(SECTIONS):
@@ -192,10 +262,11 @@
                 mid[section, i] = new
         if not last:
             src = mid.at[section]
+            copies = send_rows(section + 1, src)
             fill_edges(section + 1, src)
-            copies = start(section + 1, src)
-
-    taken = dot_n(pick, state_ref[...], HIGHEST)
+            copies += send_columns(section + 1)
+
+    taken = pick_rows(pick, state_ref[...])
     first, second = taken[:half], taken[half:]
     first = jnp.where(slot_odd[:half] < 0.5, first, pltpu.roll(first, MEMBERS, 1))
     second = jnp.where(slot_odd[half:] > 0.5, second, pltpu.roll(second, MEMBERS, 1))
@@ -275,54 +346,24 @@
     lon_n,
     state_ref,
     gather_ref,
-    rank_ref,
-    owner_ref,
-    site_ref,
-    class_ref,
-    cutoff_ref,
-    value_ref,
-    var_ref,
+    meta_ref,
     noise_ref,
     out_ref,
     x_ref,
-    noise_wide,
 ):
     tile_lat, tile_lon, width = out_ref.shape
     pairs = width // LANES
     ilat = lax.axis_index("lat")
     ilon = lax.axis_index("lon")
     lon_cells = float(tile_lon * lon_n)
-    count = owner_ref.shape[1]
+    count = meta_ref.shape[1]
     scale = 1.0 / (MEMBERS - 1)
     low_lanes = iota((count, LANES), 1) < MEMBERS
 
-    rows_of = []
-    stacked = []
-    for k in range(BATCH_GROUPS):
-        owner = owner_ref[k : k + 1, :].astype(jnp.float32)
-        site = site_ref[k : k + 1, :].astype(jnp.float32)
-        classes = class_ref[k : k + 1, :]
-        cell = floor_div(site, LEV)
-        cell_lat = floor_div(cell, tile_lon)
-        tile_row = floor_div(owner, lon_n)
-        glat = tile_row * tile_lat + cell_lat
-        glon = (owner - lon_n * tile_row) * tile_lon + cell - tile_lon * cell_lat
-        radius = jnp.zeros((1, count), jnp.float32)
-        for c in range(cutoff_ref.shape[0]):
-            radius = jnp.where(classes == c, cutoff_ref[c].astype(jnp.float32), radius)
-        slot = rank_ref[k : k + 1, :] + float(CAP * k)
-        slot_half = floor_div(slot, 2)
-        rows_of.append((glat, glon, 1.0 / radius))
-        stacked += [
-            glat,
-            glon,
-            owner * SLOT_ROWS + slot_half,
-            slot - 2.0 * slot_half,
-            value_ref[k : k + 1, :],
-            var_ref[k : k + 1, :],
-            jnp.zeros((2, count), jnp.float32),
-        ]
-    table = jnp.concatenate(stacked, axis=0).T
+    table = meta_ref[...].T
+    rows_of = [
+        [meta_ref[8 * k + n : 8 * k + n + 1, :] for n in (0, 1, 6)] for k in range(BATCH_GROUPS)
+    ]
 
     def col(k, n):
         return table[:, 8 * k + n : 8 * k + n + 1]
@@ -338,7 +379,7 @@
     priors = []
     for k in range(BATCH_GROUPS):
         pick = jnp.where(iota((count, slots), 1).astype(jnp.float32) == col(k, 2), 1.0, 0.0)
-        taken = dot_n(pick, gather_ref[...], HIGHEST)
+        taken = pick_rows(pick.astype(jnp.bfloat16), gather_ref[...])
         turned = pltpu.roll(taken, MEMBERS, 1)
         odd = col(k, 3) > 0.5
         priors.append(jnp.where(odd != low_lanes, taken, turned))
@@ -348,22 +389,21 @@
         var = col(k, 5)
         inverse_var = 1.0 / var
         anom = prior - jnp.mean(prior, axis=1, keepdims=True)
-        noise_wide[:, :MEMBERS] = noise_ref[k]
-        noise_wide[:, MEMBERS:] = noise_ref[k]
-        rhs = col(k, 4) + jnp.sqrt(var) * noise_wide[...] - prior
+        noise = jnp.concatenate([noise_ref[k], noise_ref[k]], axis=0).T
+        rhs = col(k, 4) + jnp.sqrt(var) * noise - prior
         both = inverse_var * jnp.where(low_lanes, anom, rhs)
-        aug = scale * dot_n(anom.T[:MEMBERS], both, HIGHEST)
+        aug = scale * dot3(dot_n, anom.T[:MEMBERS], both)
         aug += jnp.where(iota(aug.shape, 0) == iota(aug.shape, 1), 1.0, 0.0)
         solved = gauss_jordan(aug)
         solved = jnp.where(
             iota(solved.shape, 1) < MEMBERS, pltpu.roll(solved, MEMBERS, 1), solved
         )
-        white = inverse_var * (rhs - dot_n(anom[:, :MEMBERS], solved, HIGHEST))
+        white = inverse_var * (rhs - dot3(dot_n, anom[:, :MEMBERS], solved))
 
         for later in range(k + 1, BATCH_GROUPS):
-            cov = dot_t(priors[later][:, :MEMBERS], anom[:, :MEMBERS], HIGHEST)
+            cov = dot3(dot_t, priors[later][:, :MEMBERS], anom[:, :MEMBERS])
             cov = cov * rho_of(col(later, 0), col(later, 1), k)
-            priors[later] = priors[later] + dot_n(cov, white, HIGHEST)
+            priors[later] = priors[later] + dot3(dot_n, cov, white)
 
         wide_anom = jnp.concatenate(
             [jnp.where(low_lanes, anom, 0.0), jnp.where(low_lanes, 0.0, anom)], axis=0
@@ -419,19 +459,33 @@
     rows = tile_lat * tile_lon * width // LANES
     count = obs_site.shape[1]
     vmem = pl.BlockSpec(memory_space=pltpu.VMEM)
-    smem = pl.BlockSpec(memory_space=pltpu.SMEM)
     f32 = jnp.float32
     dma = pltpu.SemaphoreType.DMA
-    state, gathered, rank = pl.pallas_call(
+    loaded = (
+        ensemble,
+        northward_wind,
+        eastward_wind,
+        spreading_strength,
+        measurement_home_subdomain,
+        obs_site,
+        obs_class,
+        obs_value,
+        obs_var,
+        cutoff_table,
+    )
+    state, gathered, meta = pl.pallas_call(
         functools.partial(forecast_kernel, lat_n, lon_n),
         out_shape=(
             jax.ShapeDtypeStruct((rows, LANES), f32),
             jax.ShapeDtypeStruct((lat_n * lon_n * SLOT_ROWS, LANES), f32),
-            jax.ShapeDtypeStruct((8, count), f32),
+            jax.ShapeDtypeStruct((8 * BATCH_GROUPS, count), f32),
         ),
-        in_specs=[vmem] * 6,
+        in_specs=[pl.BlockSpec(memory_space=pltpu.HBM)] * len(loaded),
         out_specs=(vmem, vmem, vmem),
-        scratch_shapes=[
+        scratch_shapes=[pltpu.VMEM(a.shape, a.dtype) for a in loaded[:-1]]
+        + [
+            pltpu.SMEM(cutoff_table.shape, cutoff_table.dtype),
+            dma((len(loaded),)),
             pltpu.VMEM((SECTIONS - 1, tile_lat, tile_lon, width), f32),
             pltpu.VMEM((SECTIONS, 2, tile_lat, width), f32),
             pltpu.VMEM((SECTIONS, 2, tile_lon, width), f32),
@@ -447,33 +501,15 @@
         compiler_params=pltpu.CompilerParams(
             collective_id=0, has_side_effects=True, vmem_limit_bytes=32 << 20
         ),
-    )(
-        ensemble,
-        northward_wind,
-        eastward_wind,
-        spreading_strength,
-        measurement_home_subdomain,
-        obs_site,
-    )
+    )(*loaded)
     return pl.pallas_call(
         functools.partial(update_kernel, lat_n, lon_n),
         out_shape=jax.ShapeDtypeStruct(ensemble.shape, f32),
-        in_specs=[vmem] * 6 + [smem] + [vmem] * 3,
+        in_specs=[vmem] * 4,
         out_specs=vmem,
-        scratch_shapes=[pltpu.VMEM((rows, LANES), f32), pltpu.VMEM((count, LANES), f32)],
+        scratch_shapes=[pltpu.VMEM((rows, LANES), f32)],
         compiler_params=pltpu.CompilerParams(vmem_limit_bytes=48 << 20),
-    )(
-        state,
-        gathered,
-        rank,
-        measurement_home_subdomain,
-        obs_site,
-        obs_class,
-        cutoff_table,
-        obs_value,
-        obs_var,
-        obs_noise,
-    )
+    )(state, gathered, meta, jnp.swapaxes(obs_noise, 1, 2))
 
 
 def solution(mesh):

time: 36.7 us -> 40.8 us (1.11)
  local copies, waits for them, and re-layouts: 1.8 us -> 7.04 us
  Pallas kernels: 34.6 us -> 33.4 us
    unnamed x21 -> x22, local copies, waits for them, and re-layouts: 1.8 us -> 7.04 us
    pallas_call x1, Pallas kernels: 12.9 us -> 11.8 us  [body(): pl.pallas_call(functools.partial(update_kernel, lat_n, lon_n), out_shape=...]
where the time goes in v2:
time: 40.8 us; the launch traced here: 40.5 us
  Pallas kernels  33.4 us (82%)
  local copies, waits for them, and re-layouts  7.04 us (17%)
    pallas_call x1, Pallas kernels, body(): pl.pallas_call(functools.partial(forecast_kernel, lat_n, lon_n), out_shap...  21.7 us
    pallas_call x1, Pallas kernels, body(): pl.pallas_call(functools.partial(update_kernel, lat_n, lon_n), out_shape=...  11.8 us
    unnamed x22, local copies, waits for them, and re-layouts  7.04 us

profile of v2, /device:TPU:0, one launch (start us, length us, event | category | flops | bytes accessed | tf_op | source)
XLA Modules:
  0.0 40.5 jit_solution(10240079285755615327)
XLA Ops:
  0.0 0.0 copy-start.10
  0.0 0.7 %copy-done.10 = s32[8]{0:T(128)S(1)} copy-done((s32[8]{0:T(128)S(1)}, s32[8]{0:T(128)}, u32[]{:S(2)}) %copy-start.10) | copy-done | bytes 56
  0.7 0.0 copy-start
  0.7 0.9 %copy-done = f32[4,8,1792]{2,1,0:T(8,128)S(1)} copy-done((f32[4,8,1792]{2,1,0:T(8,128)S(1)}, f32[4,8,1792]{2,1,0:T(8,128)}, u32[]{:S(2)}) %copy-start) | copy-done | bytes 229400
  1.6 0.0 copy-start.2
  1.6 0.7 %copy-done.2 = f32[4,8]{1,0:T(4,128)S(1)} copy-done((f32[4,8]{1,0:T(4,128)S(1)}, f32[4,8]{1,0:T(4,128)}, u32[]{:S(2)}) %copy-start.2) | copy-done | bytes 152
  2.3 0.0 copy-start.3
  2.3 0.7 %copy-done.3 = f32[4,8]{1,0:T(4,128)S(1)} copy-done((f32[4,8]{1,0:T(4,128)S(1)}, f32[4,8]{1,0:T(4,128)}, u32[]{:S(2)}) %copy-start.3) | copy-done | bytes 152
  3.0 0.0 copy-start.4
  3.0 0.7 %copy-done.4 = f32[4,8]{1,0:T(4,128)S(1)} copy-done((f32[4,8]{1,0:T(4,128)S(1)}, f32[4,8]{1,0:T(4,128)}, u32[]{:S(2)}) %copy-start.4) | copy-done | bytes 152
  3.6 0.0 copy-start.5
  3.6 0.7 %copy-done.5 = s32[3,128]{1,0:T(4,128)S(1)} copy-done((s32[3,128]{1,0:T(4,128)S(1)}, s32[3,128]{1,0:T(4,128)}, u32[]{:S(2)}) %copy-start.5) | copy-done | bytes 1560
  4.3 0.0 copy-start.6
  4.3 0.7 %copy-done.6 = s32[3,128]{1,0:T(4,128)S(1)} copy-done((s32[3,128]{1,0:T(4,128)S(1)}, s32[3,128]{1,0:T(4,128)}, u32[]{:S(2)}) %copy-start.6) | copy-done | bytes 1560
  5.0 0.0 copy-start.7
  5.0 0.7 %copy-done.7 = s32[3,128]{1,0:T(4,128)S(1)} copy-done((s32[3,128]{1,0:T(4,128)S(1)}, s32[3,128]{1,0:T(4,128)}, u32[]{:S(2)}) %copy-start.7) | copy-done | bytes 1560
  5.7 0.0 copy-start.8
  5.7 0.7 %copy-done.8 = f32[3,128]{1,0:T(4,128)S(1)} copy-done((f32[3,128]{1,0:T(4,128)S(1)}, f32[3,128]{1,0:T(4,128)}, u32[]{:S(2)}) %copy-start.8) | copy-done | bytes 1560
  6.4 0.0 copy-start.9
  6.4 0.7 %copy-done.9 = f32[3,128]{1,0:T(4,128)S(1)} copy-done((f32[3,128]{1,0:T(4,128)S(1)}, f32[3,128]{1,0:T(4,128)}, u32[]{:S(2)}) %copy-start.9) | copy-done | bytes 1560
  7.1 0.0 copy-start.1
  7.1 21.7 %shard_map.109 = (f32[448,128]{1,0:T(8,128)S(1)}, f32[256,128]{1,0:T(8,128)S(1)}, f32[24,128]{1,0:T(8,128)S(1)}) custom-call(f32[4,8,1792]{2,1,0:T(8,128)S(1)} %copy-done, f32[4,8]{1,0:T(4,128)S(1)} %copy-done.2, f32[4,8]{1,0:T(4,128)S(1)} %copy-done.3, f32[4,8]{1,0:T(4,128)S(1)} %copy-done.4, s32[3,128]{1,0:T(4,128)S(1)} %copy-done.5, ...), custom_call_target="tpu_custom_call" | custom-call | tf_op jit(solution)/shard_map/pallas_call | solution.py:476
  28.7 0.0 copy-done.1
  28.7 11.8 %shard_map.110 = f32[4,8,1792]{2,1,0:T(8,128)} custom-call(f32[448,128]{1,0:T(8,128)S(1)} %get-tuple-element.8.state_ref, f32[256,128]{1,0:T(8,128)S(1)} %get-tuple-element.9.gather_ref, f32[24,128]{1,0:T(8,128)S(1)} %get-tuple-element.10.meta_ref, f32[3,64,128]{2,1,0:T(8,128)S(1)} %bitcast.1), custom_call_target="tpu_custom_call" | custom-call | tf_op jit(solution)/shard_map/pallas_call | solution.py:505
Async XLA Ops:
  0.0 0.7 %copy-start.10 = (s32[8]{0:T(128)S(1)}, s32[8]{0:T(128)}, u32[]{:S(2)}) copy-start(s32[8]{0:T(128)} %cutoff_hbm.1) | copy-start | bytes 100
  0.7 0.9 %copy-start = (f32[4,8,1792]{2,1,0:T(8,128)S(1)}, f32[4,8,1792]{2,1,0:T(8,128)}, u32[]{:S(2)}) copy-start(f32[4,8,1792]{2,1,0:T(8,128)} %ens_hbm.1) | copy-start | bytes 688132
  1.6 0.7 %copy-start.2 = (f32[4,8]{1,0:T(4,128)S(1)}, f32[4,8]{1,0:T(4,128)}, u32[]{:S(2)}) copy-start(f32[4,8]{1,0:T(4,128)} %north_hbm.1) | copy-start | bytes 388
  2.3 0.7 %copy-start.3 = (f32[4,8]{1,0:T(4,128)S(1)}, f32[4,8]{1,0:T(4,128)}, u32[]{:S(2)}) copy-start(f32[4,8]{1,0:T(4,128)} %east_hbm.1) | copy-start | bytes 388
  3.0 0.7 %copy-start.4 = (f32[4,8]{1,0:T(4,128)S(1)}, f32[4,8]{1,0:T(4,128)}, u32[]{:S(2)}) copy-start(f32[4,8]{1,0:T(4,128)} %spread_hbm.1) | copy-start | bytes 388
  3.6 0.7 %copy-start.5 = (s32[3,128]{1,0:T(4,128)S(1)}, s32[3,128]{1,0:T(4,128)}, u32[]{:S(2)}) copy-start(s32[3,128]{1,0:T(4,128)} %owner_hbm.1) | copy-start | bytes 4612
  4.3 0.7 %copy-start.6 = (s32[3,128]{1,0:T(4,128)S(1)}, s32[3,128]{1,0:T(4,128)}, u32[]{:S(2)}) copy-start(s32[3,128]{1,0:T(4,128)} %site_hbm.1) | copy-start | bytes 4612
  5.0 0.7 %copy-start.7 = (s32[3,128]{1,0:T(4,128)S(1)}, s32[3,128]{1,0:T(4,128)}, u32[]{:S(2)}) copy-start(s32[3,128]{1,0:T(4,128)} %class_hbm.1) | copy-start | bytes 4612
  5.7 0.7 %copy-start.8 = (f32[3,128]{1,0:T(4,128)S(1)}, f32[3,128]{1,0:T(4,128)}, u32[]{:S(2)}) copy-start(f32[3,128]{1,0:T(4,128)} %value_hbm.1) | copy-start | bytes 4612
  6.4 0.7 %copy-start.9 = (f32[3,128]{1,0:T(4,128)S(1)}, f32[3,128]{1,0:T(4,128)}, u32[]{:S(2)}) copy-start(f32[3,128]{1,0:T(4,128)} %var_hbm.1) | copy-start | bytes 4612
  7.1 21.7 %copy-start.1 = (f32[3,128,64]{1,2,0:T(8,128)S(1)}, f32[3,128,64]{1,2,0:T(8,128)}, u32[]{:S(2)}) copy-start(f32[3,128,64]{1,2,0:T(8,128)} %param.21) | copy-start | bytes 294916

commit v3 on v2

--- a/solution.py
+++ b/solution.py
@@ -9,7 +9,6 @@
 
 LEV = 28
 MEMBERS = 64
-SECTIONS = 2
 BATCH_GROUPS = 3
 CAP = 4
 LANES = 128
@@ -68,34 +67,26 @@
 def forecast_kernel(
     lat_n,
     lon_n,
-    ens_hbm,
-    north_hbm,
-    east_hbm,
-    spread_hbm,
-    owner_hbm,
-    site_hbm,
-    class_hbm,
-    value_hbm,
-    var_hbm,
-    cutoff_hbm,
-    state_ref,
-    gather_ref,
-    meta_ref,
     ens_ref,
+    spread_ref,
     north_ref,
     east_ref,
-    spread_ref,
     owner_ref,
     site_ref,
     class_ref,
     value_ref,
     var_ref,
     cutoff_ref,
-    load_sem,
-    mid,
+    state_ref,
+    gather_ref,
+    meta_ref,
     edge,
+    corner,
+    wind,
     halo_lat,
     halo_lon,
+    halo_corner,
+    halo_wind,
     slots,
     send_sem,
     recv_sem,
@@ -111,83 +102,72 @@
     lon_peers = [lax.rem(ilon + d, lon_n) for d in range(1, lon_n)]
     lat_peers = [lax.rem(ilat + d, lat_n) for d in range(1, lat_n)]
 
+    up = lax.rem(ilat + 1, lat_n)
+    down = lax.rem(ilat + lat_n - 1, lat_n)
+    right = lax.rem(ilon + 1, lon_n)
+    left = lax.rem(ilon + lon_n - 1, lon_n)
+    diagonal = [(up, right), (up, left), (down, right), (down, left)]
+
     barrier = pltpu.get_barrier_semaphore()
     for peer in lon_peers:
         pl.semaphore_signal(barrier, inc=1, device_id=(ilat, peer), device_id_type=MESH)
     for peer in lat_peers:
         pl.semaphore_signal(barrier, inc=1, device_id=(peer, ilon), device_id_type=MESH)
 
-    loads = []
-    for n, (a, b) in enumerate(
-        (
-            (ens_hbm, ens_ref),
-            (spread_hbm, spread_ref),
-            (north_hbm, north_ref),
-            (east_hbm, east_ref),
-            (owner_hbm, owner_ref),
-            (site_hbm, site_ref),
-            (class_hbm, class_ref),
-            (cutoff_hbm, cutoff_ref),
-            (value_hbm, value_ref),
-            (var_hbm, var_ref),
-        )
-    ):
-        load = pltpu.make_async_copy(a, b, load_sem.at[n])
-        load.start()
-        loads.append(load)
-
-    def fill_edges(section, src):
-        for i in range(tile_lat):
-            edge[section, 0, i : i + 1, :] = src[i, tile_lon - 1 : tile_lon, :]
-            edge[section, 1, i : i + 1, :] = src[i, 0:1, :]
-
-    up = lax.rem(ilat + 1, lat_n)
-    down = lax.rem(ilat + lat_n - 1, lat_n)
-    right = lax.rem(ilon + 1, lon_n)
-    left = lax.rem(ilon + lon_n - 1, lon_n)
-
-    def send(section, n, a, b, device):
+    for device in diagonal:
+        pl.semaphore_signal(barrier, inc=1, device_id=device, device_id_type=MESH)
+
+    top, end = tile_lat - 1, tile_lon - 1
+    for i in range(tile_lat):
+        for c in range(2):
+            at = c * tile_lat + i
+            edge[0, at : at + 1, :] = ens_ref[i, end - 1 + c : end + c, :]
+            edge[1, at : at + 1, :] = ens_ref[i, c : c + 1, :]
+    for n, (i, j) in enumerate(((top, end), (top, 0), (0, end), (0, 0))):
+        corner[n] = ens_ref[i, j : j + 1, :]
+    for n, ref in enumerate((spread_ref, north_ref, east_ref)):
+        wind[n] = ref[...]
+
+    pl.semaphore_wait(barrier, len(lon_peers) + len(lat_peers) + len(diagonal))
+    moves = [
+        (ens_ref.at[pl.ds(tile_lat - 2, 2)], halo_lat.at[0], (up, ilon)),
+        (ens_ref.at[pl.ds(0, 2)], halo_lat.at[1], (down, ilon)),
+        (edge.at[0], halo_lon.at[0], (ilat, right)),
+        (edge.at[1], halo_lon.at[1], (ilat, left)),
+        (wind, halo_wind.at[0], (up, ilon)),
+        (wind, halo_wind.at[1], (down, ilon)),
+        (wind, halo_wind.at[2], (ilat, right)),
+        (wind, halo_wind.at[3], (ilat, left)),
+    ] + [(corner.at[n], halo_corner.at[n], device) for n, device in enumerate(diagonal)]
+    copies = []
+    for n, (a, b, device) in enumerate(moves):
         copy = pltpu.make_async_remote_copy(
             src_ref=a,
             dst_ref=b,
-            send_sem=send_sem.at[section, n],
-            recv_sem=recv_sem.at[section, n],
+            send_sem=send_sem.at[n],
+            recv_sem=recv_sem.at[n],
             device_id=device,
             device_id_type=MESH,
         )
         copy.start()
-        return copy
-
-    def send_rows(section, src):
-        return [
-            send(section, 0, src.at[tile_lat - 1], halo_lat.at[section, 0], (up, ilon)),
-            send(section, 1, src.at[0], halo_lat.at[section, 1], (down, ilon)),
-        ]
-
-    def send_columns(section):
-        return [
-            send(section, 2, edge.at[section, 0], halo_lon.at[section, 0], (ilat, right)),
-            send(section, 3, edge.at[section, 1], halo_lon.at[section, 1], (ilat, left)),
-        ]
-
-    pl.semaphore_wait(barrier, len(lon_peers) + len(lat_peers))
-    copies = send_rows(0, ens_hbm)
-    loads[0].wait()
-    fill_edges(0, ens_ref)
-    copies += send_columns(0)
-    for load in loads[1:]:
-        load.wait()
+        copies.append(copy)
 
     same = iota((tile_lon, tile_lon), 0) == iota((tile_lon, tile_lon), 1)
-    coef = []
-    for i in range(tile_lat):
-        s, n, e = (
-            jnp.sum(jnp.where(same, ref[i : i + 1, :], 0.0), axis=1, keepdims=True)
-            for ref in (spread_ref, north_ref, east_ref)
-        )
+
+    def weights(s, n, e):
         n = advect_coef * n
         e = advect_coef * e
-        coef.append((1.0 - 4.0 * s, s - n, s + n, s - e, s + e))
+        return (1.0 - 4.0 * s, s - n, s + n, s - e, s + e)
+
+    def row_weights(rows):
+        return weights(
+            *(jnp.sum(jnp.where(same, row, 0.0), axis=1, keepdims=True) for row in rows)
+        )
+
+    coef = [
+        row_weights([ref[i : i + 1, :] for ref in (spread_ref, north_ref, east_ref)])
+        for i in range(tile_lat)
+    ]
 
     count = owner_ref.shape[1]
     me = (ilat * lon_n + ilon).astype(jnp.float32)
@@ -235,36 +215,59 @@
         iota((2 * half, rows), 1).astype(jnp.float32) == slot_row, 1.0, 0.0
     ).astype(jnp.bfloat16)
 
-    src = ens_ref
-    for section in range(SECTIONS):
-        for copy in copies:
-            copy.wait()
-        last = section == SECTIONS - 1
-        for i in range(tile_lat):
-            centre, c_n, c_s, c_e, c_w = coef[i]
-            here = src[i]
-            if i + 1 < tile_lat:
-                above = src[i + 1]
-            else:
-                above = jnp.where(ilat == lat_n - 1, 0.0, halo_lat[section, 1])
-            if i > 0:
-                below = src[i - 1]
-            else:
-                below = jnp.where(ilat == 0, 0.0, halo_lat[section, 0])
-            east = jnp.concatenate([here[1:], halo_lon[section, 1, i : i + 1, :]], axis=0)
-            west = jnp.concatenate([halo_lon[section, 0, i : i + 1, :], here[:-1]], axis=0)
-            new = centre * here + c_n * above + c_s * below + c_e * east + c_w * west
-            if last:
-                for p in range(pairs):
-                    at = (i * pairs + p) * tile_lon
-                    state_ref[at : at + tile_lon, :] = new[:, p * LANES : (p + 1) * LANES]
-            else:
-                mid[section, i] = new
-        if not last:
-            src = mid.at[section]
-            copies = send_rows(section + 1, src)
-            fill_edges(section + 1, src)
-            copies += send_columns(section + 1)
+    for copy in copies:
+        copy.wait()
+
+    def advance(weight, here, above, below, east, west):
+        centre, c_n, c_s, c_e, c_w = weight
+        return centre * here + c_n * above + c_s * below + c_e * east + c_w * west
+
+    def along_row(weight, here, above, below, east_end, west_end):
+        east = jnp.concatenate([here[1:], east_end], axis=0)
+        west = jnp.concatenate([west_end, here[:-1]], axis=0)
+        return advance(weight, here, above, below, east, west)
+
+    first_tile, last_tile = ilat == 0, ilat == lat_n - 1
+    below_1, below_2 = (jnp.where(first_tile, 0.0, halo_lat[0, n]) for n in (1, 0))
+    above_1, above_2 = (jnp.where(last_tile, 0.0, halo_lat[1, n]) for n in (0, 1))
+    corner_bw, corner_be = (jnp.where(first_tile, 0.0, halo_corner[n]) for n in (0, 1))
+    corner_aw, corner_ae = (jnp.where(last_tile, 0.0, halo_corner[n]) for n in (2, 3))
+    west_2, west_1 = halo_lon[0, :tile_lat], halo_lon[0, tile_lat:]
+    east_1, east_2 = halo_lon[1, :tile_lat], halo_lon[1, tile_lat:]
+    own_east, own_west = edge[0, tile_lat:], edge[1, :tile_lat]
+
+    rows = [below_1] + [ens_ref[i] for i in range(tile_lat)] + [above_1]
+    mid = [
+        along_row(
+            coef[i], rows[i + 1], rows[i + 2], rows[i], east_1[i : i + 1], west_1[i : i + 1]
+        )
+        for i in range(tile_lat)
+    ]
+    weight = row_weights([halo_wind[0, n, top : top + 1, :] for n in range(3)])
+    mid_below = along_row(weight, below_1, rows[1], below_2, corner_be, corner_bw)
+    weight = row_weights([halo_wind[1, n, 0:1, :] for n in range(3)])
+    mid_above = along_row(weight, above_1, above_2, rows[tile_lat], corner_ae, corner_aw)
+    mid_below = jnp.where(first_tile, 0.0, mid_below)
+    mid_above = jnp.where(last_tile, 0.0, mid_above)
+
+    def along_column(weight, here, above_end, below_end, east, west):
+        above = jnp.concatenate([here[1:], above_end], axis=0)
+        below = jnp.concatenate([below_end, here[:-1]], axis=0)
+        return advance(weight, here, above, below, east, west)
+
+    weight = weights(*(halo_wind[2, n, :, end : end + 1] for n in range(3)))
+    mid_west = along_column(weight, west_1, corner_aw, corner_bw, own_west, west_2)
+    weight = weights(*(halo_wind[3, n, :, 0:1] for n in range(3)))
+    mid_east = along_column(weight, east_1, corner_ae, corner_be, east_2, own_east)
+
+    rows = [mid_below] + mid + [mid_above]
+    for i in range(tile_lat):
+        new = along_row(
+            coef[i], rows[i + 1], rows[i + 2], rows[i], mid_east[i : i + 1], mid_west[i : i + 1]
+        )
+        for p in range(pairs):
+            at = (i * pairs + p) * tile_lon
+            state_ref[at : at + tile_lon, :] = new[:, p * LANES : (p + 1) * LANES]
 
     taken = pick_rows(pick, state_ref[...])
     first, second = taken[:half], taken[half:]
@@ -463,9 +466,9 @@
     dma = pltpu.SemaphoreType.DMA
     loaded = (
         ensemble,
+        spreading_strength,
         northward_wind,
         eastward_wind,
-        spreading_strength,
         measurement_home_subdomain,
         obs_site,
         obs_class,
@@ -480,19 +483,19 @@
             jax.ShapeDtypeStruct((lat_n * lon_n * SLOT_ROWS, LANES), f32),
             jax.ShapeDtypeStruct((8 * BATCH_GROUPS, count), f32),
         ),
-        in_specs=[pl.BlockSpec(memory_space=pltpu.HBM)] * len(loaded),
+        in_specs=[vmem] * (len(loaded) - 1) + [pl.BlockSpec(memory_space=pltpu.SMEM)],
         out_specs=(vmem, vmem, vmem),
-        scratch_shapes=[pltpu.VMEM(a.shape, a.dtype) for a in loaded[:-1]]
-        + [
-            pltpu.SMEM(cutoff_table.shape, cutoff_table.dtype),
-            dma((len(loaded),)),
-            pltpu.VMEM((SECTIONS - 1, tile_lat, tile_lon, width), f32),
-            pltpu.VMEM((SECTIONS, 2, tile_lat, width), f32),
-            pltpu.VMEM((SECTIONS, 2, tile_lon, width), f32),
-            pltpu.VMEM((SECTIONS, 2, tile_lat, width), f32),
+        scratch_shapes=[
+            pltpu.VMEM((2, 2 * tile_lat, width), f32),
+            pltpu.VMEM((4, 1, width), f32),
+            pltpu.VMEM((3, tile_lat, tile_lon), f32),
+            pltpu.VMEM((2, 2, tile_lon, width), f32),
+            pltpu.VMEM((2, 2 * tile_lat, width), f32),
+            pltpu.VMEM((4, 1, width), f32),
+            pltpu.VMEM((4, 3, tile_lat, tile_lon), f32),
             pltpu.VMEM((lat_n, lon_n, SLOT_ROWS, LANES), f32),
-            dma((SECTIONS, 4)),
-            dma((SECTIONS, 4)),
+            dma((12,)),
+            dma((12,)),
             dma((lon_n - 1,)),
             dma((lon_n - 1,)),
             dma((lat_n - 1,)),

time: 40.8 us -> 41.5 us (1.017)
  Pallas kernels: 33.4 us -> 34.1 us
    pallas_call x1, Pallas kernels: 21.7 us -> 22.3 us  [body(): pl.pallas_call(functools.partial(forecast_kernel, lat_n, lon_n), out_shap...]
where the time goes in v3:
time: 41.5 us; the launch traced here: 41.1 us
  Pallas kernels  34.1 us (82%)
  local copies, waits for them, and re-layouts  7.04 us (17%)
    pallas_call x1, Pallas kernels, body(): pl.pallas_call(functools.partial(forecast_kernel, lat_n, lon_n), out_shap...  22.3 us
    pallas_call x1, Pallas kernels, body(): pl.pallas_call(functools.partial(update_kernel, lat_n, lon_n), out_shape=...  11.7 us
    unnamed x22, local copies, waits for them, and re-layouts  7.04 us

profile of v3, /device:TPU:0, one launch (start us, length us, event | category | flops | bytes accessed | tf_op | source)
XLA Modules:
  0.0 41.1 jit_solution(2539421412182253502)
XLA Ops:
  0.0 0.0 copy-start.10
  0.0 0.7 %copy-done.10 = s32[8]{0:T(128)S(1)} copy-done((s32[8]{0:T(128)S(1)}, s32[8]{0:T(128)}, u32[]{:S(2)}) %copy-start.10) | copy-done | bytes 56
  0.7 0.0 copy-start
  0.7 0.9 %copy-done = f32[4,8,1792]{2,1,0:T(8,128)S(1)} copy-done((f32[4,8,1792]{2,1,0:T(8,128)S(1)}, f32[4,8,1792]{2,1,0:T(8,128)}, u32[]{:S(2)}) %copy-start) | copy-done | bytes 229400
  1.6 0.0 copy-start.2
  1.6 0.7 %copy-done.2 = f32[4,8]{1,0:T(4,128)S(1)} copy-done((f32[4,8]{1,0:T(4,128)S(1)}, f32[4,8]{1,0:T(4,128)}, u32[]{:S(2)}) %copy-start.2) | copy-done | bytes 152
  2.3 0.0 copy-start.3
  2.3 0.7 %copy-done.3 = f32[4,8]{1,0:T(4,128)S(1)} copy-done((f32[4,8]{1,0:T(4,128)S(1)}, f32[4,8]{1,0:T(4,128)}, u32[]{:S(2)}) %copy-start.3) | copy-done | bytes 152
  3.0 0.0 copy-start.4
  3.0 0.7 %copy-done.4 = f32[4,8]{1,0:T(4,128)S(1)} copy-done((f32[4,8]{1,0:T(4,128)S(1)}, f32[4,8]{1,0:T(4,128)}, u32[]{:S(2)}) %copy-start.4) | copy-done | bytes 152
  3.6 0.0 copy-start.5
  3.6 0.7 %copy-done.5 = s32[3,128]{1,0:T(4,128)S(1)} copy-done((s32[3,128]{1,0:T(4,128)S(1)}, s32[3,128]{1,0:T(4,128)}, u32[]{:S(2)}) %copy-start.5) | copy-done | bytes 1560
  4.3 0.0 copy-start.6
  4.3 0.7 %copy-done.6 = s32[3,128]{1,0:T(4,128)S(1)} copy-done((s32[3,128]{1,0:T(4,128)S(1)}, s32[3,128]{1,0:T(4,128)}, u32[]{:S(2)}) %copy-start.6) | copy-done | bytes 1560
  5.0 0.0 copy-start.7
  5.0 0.7 %copy-done.7 = s32[3,128]{1,0:T(4,128)S(1)} copy-done((s32[3,128]{1,0:T(4,128)S(1)}, s32[3,128]{1,0:T(4,128)}, u32[]{:S(2)}) %copy-start.7) | copy-done | bytes 1560
  5.7 0.0 copy-start.8
  5.7 0.7 %copy-done.8 = f32[3,128]{1,0:T(4,128)S(1)} copy-done((f32[3,128]{1,0:T(4,128)S(1)}, f32[3,128]{1,0:T(4,128)}, u32[]{:S(2)}) %copy-start.8) | copy-done | bytes 1560
  6.4 0.0 copy-start.9
  6.4 0.7 %copy-done.9 = f32[3,128]{1,0:T(4,128)S(1)} copy-done((f32[3,128]{1,0:T(4,128)S(1)}, f32[3,128]{1,0:T(4,128)}, u32[]{:S(2)}) %copy-start.9) | copy-done | bytes 1560
  7.1 0.0 copy-start.1
  7.1 22.3 %shard_map.109 = (f32[448,128]{1,0:T(8,128)S(1)}, f32[256,128]{1,0:T(8,128)S(1)}, f32[24,128]{1,0:T(8,128)S(1)}) custom-call(f32[4,8,1792]{2,1,0:T(8,128)S(1)} %copy-done, f32[4,8]{1,0:T(4,128)S(1)} %copy-done.2, f32[4,8]{1,0:T(4,128)S(1)} %copy-done.3, f32[4,8]{1,0:T(4,128)S(1)} %copy-done.4, s32[3,128]{1,0:T(4,128)S(1)} %copy-done.5, ...), custom_call_target="tpu_custom_call" | custom-call | tf_op jit(solution)/shard_map/pallas_call | solution.py:479
  29.4 0.0 copy-done.1
  29.4 11.7 %shard_map.110 = f32[4,8,1792]{2,1,0:T(8,128)} custom-call(f32[448,128]{1,0:T(8,128)S(1)} %get-tuple-element.8.state_ref, f32[256,128]{1,0:T(8,128)S(1)} %get-tuple-element.9.gather_ref, f32[24,128]{1,0:T(8,128)S(1)} %get-tuple-element.10.meta_ref, f32[3,64,128]{2,1,0:T(8,128)S(1)} %bitcast.1), custom_call_target="tpu_custom_call" | custom-call | tf_op jit(solution)/shard_map/pallas_call | solution.py:508
Async XLA Ops:
  0.0 0.7 %copy-start.10 = (s32[8]{0:T(128)S(1)}, s32[8]{0:T(128)}, u32[]{:S(2)}) copy-start(s32[8]{0:T(128)} %cutoff_ref.1) | copy-start | bytes 100
  0.7 0.9 %copy-start = (f32[4,8,1792]{2,1,0:T(8,128)S(1)}, f32[4,8,1792]{2,1,0:T(8,128)}, u32[]{:S(2)}) copy-start(f32[4,8,1792]{2,1,0:T(8,128)} %ens_ref.1) | copy-start | bytes 688132
  1.6 0.7 %copy-start.2 = (f32[4,8]{1,0:T(4,128)S(1)}, f32[4,8]{1,0:T(4,128)}, u32[]{:S(2)}) copy-start(f32[4,8]{1,0:T(4,128)} %spread_ref.1) | copy-start | bytes 388
  2.3 0.7 %copy-start.3 = (f32[4,8]{1,0:T(4,128)S(1)}, f32[4,8]{1,0:T(4,128)}, u32[]{:S(2)}) copy-start(f32[4,8]{1,0:T(4,128)} %north_ref.1) | copy-start | bytes 388
  3.0 0.7 %copy-start.4 = (f32[4,8]{1,0:T(4,128)S(1)}, f32[4,8]{1,0:T(4,128)}, u32[]{:S(2)}) copy-start(f32[4,8]{1,0:T(4,128)} %east_ref.1) | copy-start | bytes 388
  3.6 0.7 %copy-start.5 = (s32[3,128]{1,0:T(4,128)S(1)}, s32[3,128]{1,0:T(4,128)}, u32[]{:S(2)}) copy-start(s32[3,128]{1,0:T(4,128)} %owner_ref.1) | copy-start | bytes 4612
  4.3 0.7 %copy-start.6 = (s32[3,128]{1,0:T(4,128)S(1)}, s32[3,128]{1,0:T(4,128)}, u32[]{:S(2)}) copy-start(s32[3,128]{1,0:T(4,128)} %site_ref.1) | copy-start | bytes 4612
  5.0 0.7 %copy-start.7 = (s32[3,128]{1,0:T(4,128)S(1)}, s32[3,128]{1,0:T(4,128)}, u32[]{:S(2)}) copy-start(s32[3,128]{1,0:T(4,128)} %class_ref.1) | copy-start | bytes 4612
  5.7 0.7 %copy-start.8 = (f32[3,128]{1,0:T(4,128)S(1)}, f32[3,128]{1,0:T(4,128)}, u32[]{:S(2)}) copy-start(f32[3,128]{1,0:T(4,128)} %value_ref.1) | copy-start | bytes 4612
  6.4 0.7 %copy-start.9 = (f32[3,128]{1,0:T(4,128)S(1)}, f32[3,128]{1,0:T(4,128)}, u32[]{:S(2)}) copy-start(f32[3,128]{1,0:T(4,128)} %var_ref.1) | copy-start | bytes 4612
  7.1 22.3 %copy-start.1 = (f32[3,128,64]{1,2,0:T(8,128)S(1)}, f32[3,128,64]{1,2,0:T(8,128)}, u32[]{:S(2)}) copy-start(f32[3,128,64]{1,2,0:T(8,128)} %param.21) | copy-start | bytes 294916

commit v4 on v3

--- a/solution.py
+++ b/solution.py
@@ -67,6 +67,19 @@
 def forecast_kernel(
     lat_n,
     lon_n,
+    ens_any,
+    spread_any,
+    north_any,
+    east_any,
+    owner_any,
+    site_any,
+    class_any,
+    value_any,
+    var_any,
+    cutoff_any,
+    state_ref,
+    gather_ref,
+    meta_ref,
     ens_ref,
     spread_ref,
     north_ref,
@@ -77,9 +90,7 @@
     value_ref,
     var_ref,
     cutoff_ref,
-    state_ref,
-    gather_ref,
-    meta_ref,
+    load_sem,
     edge,
     corner,
     wind,
@@ -117,6 +128,27 @@
     for device in diagonal:
         pl.semaphore_signal(barrier, inc=1, device_id=device, device_id_type=MESH)
 
+    loads = []
+    for n, (a, b) in enumerate(
+        (
+            (ens_any, ens_ref),
+            (spread_any, spread_ref),
+            (north_any, north_ref),
+            (east_any, east_ref),
+            (owner_any, owner_ref),
+            (site_any, site_ref),
+            (class_any, class_ref),
+            (value_any, value_ref),
+            (var_any, var_ref),
+            (cutoff_any, cutoff_ref),
+        )
+    ):
+        load = pltpu.make_async_copy(a, b, load_sem.at[n])
+        load.start()
+        loads.append(load)
+    for load in loads:
+        load.wait()
+
     top, end = tile_lat - 1, tile_lon - 1
     for i in range(tile_lat):
         for c in range(2):
@@ -129,18 +161,23 @@
         wind[n] = ref[...]
 
     pl.semaphore_wait(barrier, len(lon_peers) + len(lat_peers) + len(diagonal))
+    first_tile, last_tile = ilat == 0, ilat == lat_n - 1
     moves = [
-        (ens_ref.at[pl.ds(tile_lat - 2, 2)], halo_lat.at[0], (up, ilon)),
-        (ens_ref.at[pl.ds(0, 2)], halo_lat.at[1], (down, ilon)),
-        (edge.at[0], halo_lon.at[0], (ilat, right)),
-        (edge.at[1], halo_lon.at[1], (ilat, left)),
-        (wind, halo_wind.at[0], (up, ilon)),
-        (wind, halo_wind.at[1], (down, ilon)),
-        (wind, halo_wind.at[2], (ilat, right)),
-        (wind, halo_wind.at[3], (ilat, left)),
-    ] + [(corner.at[n], halo_corner.at[n], device) for n, device in enumerate(diagonal)]
+        (ens_ref.at[pl.ds(tile_lat - 2, 2)], halo_lat.at[0], (up, ilon), last_tile, first_tile),
+        (ens_ref.at[pl.ds(0, 2)], halo_lat.at[1], (down, ilon), first_tile, last_tile),
+        (edge.at[0], halo_lon.at[0], (ilat, right), None, None),
+        (edge.at[1], halo_lon.at[1], (ilat, left), None, None),
+        (wind, halo_wind.at[0], (up, ilon), last_tile, first_tile),
+        (wind, halo_wind.at[1], (down, ilon), first_tile, last_tile),
+        (wind, halo_wind.at[2], (ilat, right), None, None),
+        (wind, halo_wind.at[3], (ilat, left), None, None),
+        (corner.at[0], halo_corner.at[0], diagonal[0], last_tile, first_tile),
+        (corner.at[1], halo_corner.at[1], diagonal[1], last_tile, first_tile),
+        (corner.at[2], halo_corner.at[2], diagonal[2], first_tile, last_tile),
+        (corner.at[3], halo_corner.at[3], diagonal[3], first_tile, last_tile),
+    ]
     copies = []
-    for n, (a, b, device) in enumerate(moves):
+    for n, (a, b, device, no_send, no_recv) in enumerate(moves):
         copy = pltpu.make_async_remote_copy(
             src_ref=a,
             dst_ref=b,
@@ -149,8 +186,11 @@
             device_id=device,
             device_id_type=MESH,
         )
-        copy.start()
-        copies.append(copy)
+        copies.append((copy, no_send, no_recv))
+        if no_send is None:
+            copy.start()
+        else:
+            pl.when(jnp.logical_not(no_send))(copy.start)
 
     same = iota((tile_lon, tile_lon), 0) == iota((tile_lon, tile_lon), 1)
 
@@ -215,8 +255,12 @@
         iota((2 * half, rows), 1).astype(jnp.float32) == slot_row, 1.0, 0.0
     ).astype(jnp.bfloat16)
 
-    for copy in copies:
-        copy.wait()
+    for copy, no_send, no_recv in copies:
+        if no_send is None:
+            copy.wait()
+        else:
+            pl.when(jnp.logical_not(no_send))(copy.wait_send)
+            pl.when(jnp.logical_not(no_recv))(copy.wait_recv)
 
     def advance(weight, here, above, below, east, west):
         centre, c_n, c_s, c_e, c_w = weight
@@ -227,7 +271,6 @@
         west = jnp.concatenate([west_end, here[:-1]], axis=0)
         return advance(weight, here, above, below, east, west)
 
-    first_tile, last_tile = ilat == 0, ilat == lat_n - 1
     below_1, below_2 = (jnp.where(first_tile, 0.0, halo_lat[0, n]) for n in (1, 0))
     above_1, above_2 = (jnp.where(last_tile, 0.0, halo_lat[1, n]) for n in (0, 1))
     corner_bw, corner_be = (jnp.where(first_tile, 0.0, halo_corner[n]) for n in (0, 1))
@@ -483,9 +526,12 @@
             jax.ShapeDtypeStruct((lat_n * lon_n * SLOT_ROWS, LANES), f32),
             jax.ShapeDtypeStruct((8 * BATCH_GROUPS, count), f32),
         ),
-        in_specs=[vmem] * (len(loaded) - 1) + [pl.BlockSpec(memory_space=pltpu.SMEM)],
+        in_specs=[pl.BlockSpec(memory_space=pl.ANY)] * len(loaded),
         out_specs=(vmem, vmem, vmem),
-        scratch_shapes=[
+        scratch_shapes=[pltpu.VMEM(a.shape, a.dtype) for a in loaded[:-1]]
+        + [
+            pltpu.SMEM(cutoff_table.shape, cutoff_table.dtype),
+            dma((len(loaded),)),
             pltpu.VMEM((2, 2 * tile_lat, width), f32),
             pltpu.VMEM((4, 1, width), f32),
             pltpu.VMEM((3, tile_lat, tile_lon), f32),
@@ -502,7 +548,7 @@
             dma((lat_n - 1,)),
         ],
         compiler_params=pltpu.CompilerParams(
-            collective_id=0, has_side_effects=True, vmem_limit_bytes=32 << 20
+            collective_id=0, has_side_effects=True, vmem_limit_bytes=63 << 20
         ),
     )(*loaded)
     return pl.pallas_call(
@@ -511,7 +557,7 @@
         in_specs=[vmem] * 4,
         out_specs=vmem,
         scratch_shapes=[pltpu.VMEM((rows, LANES), f32)],
-        compiler_params=pltpu.CompilerParams(vmem_limit_bytes=48 << 20),
+        compiler_params=pltpu.CompilerParams(vmem_limit_bytes=63 << 20),
     )(state, gathered, meta, jnp.swapaxes(obs_noise, 1, 2))
 
 

time: 41.5 us -> 35 us (0.84)
  local copies, waits for them, and re-layouts: 7.04 us -> 0 us
  Pallas kernels: 34.1 us -> 34.8 us
    unnamed x22 -> x0, local copies, waits for them, and re-layouts: 7.04 us -> none
    pallas_call x1, Pallas kernels: 11.7 us -> 12.8 us  [body(): pl.pallas_call(functools.partial(update_kernel, lat_n, lon_n), out_shape=...]
where the time goes in v4:
time: 35 us; the launch traced here: 34.8 us
  Pallas kernels  34.8 us (99%)
    pallas_call x1, Pallas kernels, body(): pl.pallas_call(functools.partial(forecast_kernel, lat_n, lon_n), out_shap...  22 us
    pallas_call x1, Pallas kernels, body(): pl.pallas_call(functools.partial(update_kernel, lat_n, lon_n), out_shape=...  12.8 us

profile of v4, /device:TPU:0, one launch (start us, length us, event | category | flops | bytes accessed | tf_op | source)
XLA Modules:
  0.0 34.8 jit_solution(365736904269220438)
XLA Ops:
  0.0 22.0 %shard_map.109 = (f32[448,128]{1,0:T(8,128)}, f32[256,128]{1,0:T(8,128)}, f32[24,128]{1,0:T(8,128)}) custom-call(f32[4,8,1792]{2,1,0:T(8,128)} %ens_any.1, f32[4,8]{1,0:T(4,128)} %spread_any.1, f32[4,8]{1,0:T(4,128)} %north_any.1, f32[4,8]{1,0:T(4,128)} %east_any.1, s32[3,128]{1,0:T(4,128)} %owner_any.1, s32[3,128]{1,0:T(4,128)} %site_any.1, ...), custom_call_target="tpu_custom_call" | custom-call | tf_op jit(solution)/shard_map/pallas_call | solution.py:522
  22.0 12.8 %shard_map.110 = f32[4,8,1792]{2,1,0:T(8,128)} custom-call(f32[448,128]{1,0:T(8,128)} %get-tuple-element.8.state_ref, f32[256,128]{1,0:T(8,128)} %get-tuple-element.9.gather_ref, f32[24,128]{1,0:T(8,128)} %get-tuple-element.10.meta_ref, f32[3,64,128]{2,1,0:T(8,128)} %bitcast.1), custom_call_target="tpu_custom_call" | custom-call | tf_op jit(solution)/shard_map/pallas_call | solution.py:554

commit v5 on v4

--- a/solution.py
+++ b/solution.py
@@ -12,7 +12,7 @@
 BATCH_GROUPS = 3
 CAP = 4
 LANES = 128
-PIVOTS = 4
+PIVOTS = 8
 
 advect_coef = 0.2
 MESH = pl.DeviceIdType.MESH

time: 35 us -> 33.9 us (0.969)
  Pallas kernels: 34.8 us -> 33.7 us
    pallas_call x1, Pallas kernels: 12.8 us -> 11.8 us  [body(): pl.pallas_call(functools.partial(update_kernel, lat_n, lon_n), out_shape=...]
where the time goes in v5:
time: 33.9 us; the launch traced here: 33.8 us
  Pallas kernels  33.7 us (99%)
    pallas_call x1, Pallas kernels, body(): pl.pallas_call(functools.partial(forecast_kernel, lat_n, lon_n), out_shap...  22 us
    pallas_call x1, Pallas kernels, body(): pl.pallas_call(functools.partial(update_kernel, lat_n, lon_n), out_shape=...  11.8 us

profile of v5, /device:TPU:0, one launch (start us, length us, event | category | flops | bytes accessed | tf_op | source)
XLA Modules:
  0.0 33.8 jit_solution(1883277085181142311)
XLA Ops:
  0.0 22.0 %shard_map.109 = (f32[448,128]{1,0:T(8,128)}, f32[256,128]{1,0:T(8,128)}, f32[24,128]{1,0:T(8,128)}) custom-call(f32[4,8,1792]{2,1,0:T(8,128)} %ens_any.1, f32[4,8]{1,0:T(4,128)} %spread_any.1, f32[4,8]{1,0:T(4,128)} %north_any.1, f32[4,8]{1,0:T(4,128)} %east_any.1, s32[3,128]{1,0:T(4,128)} %owner_any.1, s32[3,128]{1,0:T(4,128)} %site_any.1, ...), custom_call_target="tpu_custom_call" | custom-call | tf_op jit(solution)/shard_map/pallas_call | solution.py:522
  22.0 11.8 %shard_map.110 = f32[4,8,1792]{2,1,0:T(8,128)} custom-call(f32[448,128]{1,0:T(8,128)} %get-tuple-element.8.state_ref, f32[256,128]{1,0:T(8,128)} %get-tuple-element.9.gather_ref, f32[24,128]{1,0:T(8,128)} %get-tuple-element.10.meta_ref, f32[3,64,128]{2,1,0:T(8,128)} %bitcast.1), custom_call_target="tpu_custom_call" | custom-call | tf_op jit(solution)/shard_map/pallas_call | solution.py:554
